TPU v7x, 512 devices: a whole 4x8x8 slice. The times are simulated.
512 devices in a mesh: space: 128 (over x, y, z_lo), vz: 4 (over z_hi, core).
Axes of the slice: x: 4, y: 8, z: 8 (z_hi: 2, z_lo: 4; z = z_hi * 4 + z_lo), core: 2. Of those that a mesh axis runs over, the one named last changes fastest.
Arguments:
- distribution: float32 [48, 256, 8, 2304], P('vz', 'space'), may hold values from 0 to 6, as said below
- collision_rate: float32 [256, 8], P('space'), may hold values from 0.5 to 2
Outputs:
- new_distribution: float32 [48, 256, 8, 2304], P('vz', 'space')
Inputs may be any that keep to these rules, and one draw needn't show every extreme that they name: `distribution`: every entry is positive.
All inputs are finite; a program needn't handle non-finite values.
Results may differ from a plain program's by a relative error of at most 0.000056.
Values sent between devices are 32-bit elements; how exact they have to be, the bound alone decides.
No kernel may reach another device: no remote copies, remote signals or barrier semaphores. Data moves between devices by JAX's collectives and lax.ppermute only.
A program may use at most 64 MiB of HBM per device.

v0:
```python
import jax
import jax.numpy as jnp
from jax import lax
from jax.sharding import PartitionSpec as P

V = 48
SWEEPS = 3


vel_max = 4.5
step_ratio = 0.1
collision_scale = 0.004
relax_scale = 0.5


def with_halo(block, sides, width, periodic):
    for axis, dim in sides:
        count = lax.axis_size(axis)
        forward = [(i, i + 1) for i in range(count - 1)]
        if periodic:
            forward.append((count - 1, 0))
        backward = [(target, source) for source, target in forward]
        low = lax.ppermute(
            lax.slice_in_dim(block, block.shape[dim] - width, None, axis=dim), axis, forward
        )
        high = lax.ppermute(lax.slice_in_dim(block, 0, width, axis=dim), axis, backward)
        block = jnp.concatenate([low, block, high], axis=dim)
    return block


def grid_speeds(position):
    return vel_max * (2.0 * position + 1.0 - V) / V


def velocity_columns():
    grid_values = grid_speeds(jnp.arange(V, dtype=jnp.float32))
    return (jnp.repeat(grid_values, V), jnp.tile(grid_values, V))


def beam_warming(middle, near_cells, far_cells, magnitude):
    return (
        middle
        - 0.5 * magnitude * (3.0 * middle - 4.0 * near_cells + far_cells)
        + 0.5 * magnitude * magnitude * (middle - 2.0 * near_cells + far_cells)
    )


def roll_transport(field_data, speed_cols, axis_id):
    positive = speed_cols > 0
    near_cells = jnp.where(
        positive, jnp.roll(field_data, 1, axis_id), jnp.roll(field_data, -1, axis_id)
    )
    far_cells = jnp.where(
        positive, jnp.roll(field_data, 2, axis_id), jnp.roll(field_data, -2, axis_id)
    )
    return beam_warming(field_data, near_cells, far_cells, step_ratio * jnp.abs(speed_cols))


def combine_planes(partial_value, vertical_speeds):
    zero_moment = partial_value[0]
    return jnp.stack(
        [
            jnp.sum(zero_moment, 0),
            jnp.sum(partial_value[1], 0),
            jnp.sum(partial_value[2], 0),
            jnp.sum(vertical_speeds * zero_moment, 0),
            jnp.sum(partial_value[3] + vertical_speeds * vertical_speeds * zero_moment, 0),
        ]
    )


def cell_state(moment_totals):
    grid_spacing = 2.0 * vel_max / V
    unnormalised_mass = moment_totals[0]
    drift_velocity_x = moment_totals[1] / unnormalised_mass
    drift_velocity_y = moment_totals[2] / unnormalised_mass
    drift_velocity_z = moment_totals[3] / unnormalised_mass
    thermal_energy = (
        moment_totals[4] / unnormalised_mass
        - drift_velocity_x * drift_velocity_x
        - drift_velocity_y * drift_velocity_y
        - drift_velocity_z * drift_velocity_z
    ) / 3.0
    return (
        unnormalised_mass * grid_spacing**3,
        drift_velocity_x,
        drift_velocity_y,
        drift_velocity_z,
        thermal_energy,
    )


def maxwellian(cell_entries, velocity_x_grid, velocity_y_grid, vertical_speeds):
    mass_density, drift_velocity_x, drift_velocity_y, drift_velocity_z, thermal_energy = (
        cell_entries
    )
    squared_spread = (
        (velocity_x_grid - drift_velocity_x) ** 2
        + (velocity_y_grid - drift_velocity_y) ** 2
        + (vertical_speeds - drift_velocity_z) ** 2
    )
    return (
        mass_density
        * (2.0 * jnp.pi * thermal_energy) ** (-1.5)
        * jnp.exp(-squared_spread / (2.0 * thermal_energy))
    )


def velocity_shifts(middle):
    zero_row = jnp.zeros(middle.shape[:-1] + (V,), middle.dtype)
    zero_one = jnp.zeros(middle.shape[:-1] + (1,), middle.dtype)
    upper_x_neighbour = jnp.concatenate([middle[..., V:], zero_row], axis=-1)
    lower_x_neighbour = jnp.concatenate([zero_row, middle[..., :-V]], axis=-1)
    upper_y_neighbour = jnp.concatenate([middle[..., 1:], zero_one], axis=-1)
    lower_y_neighbour = jnp.concatenate([zero_one, middle[..., :-1]], axis=-1)
    return (upper_x_neighbour, lower_x_neighbour, upper_y_neighbour, lower_y_neighbour)


def relaxation_pass(
    bordered_grid,
    forcing_term,
    diagonal_factor,
    vertical_speeds,
    cell_entries,
    collide_rate,
    velocity_x_grid,
    velocity_y_grid,
    upper_mask,
    lower_mask,
):
    mass_density, drift_velocity_x, drift_velocity_y, drift_velocity_z, thermal_energy = (
        cell_entries
    )
    grid_spacing = 2.0 * vel_max / V
    stiffness_factor = thermal_energy / (grid_spacing * grid_spacing)
    half_timestep = 0.5 / grid_spacing
    middle = bordered_grid[1:-1]
    upper_x_neighbour, lower_x_neighbour, upper_y_neighbour, lower_y_neighbour = velocity_shifts(
        middle
    )
    running_total = forcing_term + collide_rate * (
        (stiffness_factor + (velocity_x_grid + grid_spacing - drift_velocity_x) * half_timestep)
        * upper_x_neighbour
        + (stiffness_factor - (velocity_x_grid - grid_spacing - drift_velocity_x) * half_timestep)
        * lower_x_neighbour
    )
    running_total = running_total + collide_rate * (
        (stiffness_factor + (velocity_y_grid + grid_spacing - drift_velocity_y) * half_timestep)
        * upper_mask
        * upper_y_neighbour
        + (stiffness_factor - (velocity_y_grid - grid_spacing - drift_velocity_y) * half_timestep)
        * lower_mask
        * lower_y_neighbour
    )
    running_total = running_total + collide_rate * (
        (stiffness_factor + (vertical_speeds + grid_spacing - drift_velocity_z) * half_timestep)
        * bordered_grid[2:]
        + (stiffness_factor - (vertical_speeds - grid_spacing - drift_velocity_z) * half_timestep)
        * bordered_grid[:-2]
    )
    return running_total / diagonal_factor


def shards(distribution, collision_rate):
    plane_count, column_count, row_count, velocity_width = distribution.shape
    half_width = velocity_width // 2
    velocity_x_grid, velocity_y_grid = velocity_columns()
    magnitude = step_ratio * jnp.abs(velocity_x_grid)
    extended = with_halo(distribution, (("space", 1),), 2, True)
    forward = beam_warming(
        distribution[..., half_width:],
        extended[:, 1 : column_count + 1, :, half_width:],
        extended[:, :column_count, :, half_width:],
        magnitude[half_width:],
    )
    backward = beam_warming(
        distribution[..., :half_width],
        extended[:, 3 : column_count + 3, :, :half_width],
        extended[:, 4 : column_count + 4, :, :half_width],
        magnitude[:half_width],
    )
    swept_x = jnp.concatenate([backward, forward], axis=-1)
    transported = roll_transport(swept_x, velocity_y_grid, 2)
    weights = jnp.stack(
        [
            jnp.ones_like(velocity_x_grid),
            velocity_x_grid,
            velocity_y_grid,
            velocity_x_grid * velocity_x_grid + velocity_y_grid * velocity_y_grid,
        ],
        axis=1,
    )
    partial_value = jnp.einsum(
        "zxyk,kw->wzxy", distribution, weights, precision=lax.Precision.HIGHEST
    )
    first_plane = lax.axis_index("vz") * plane_count
    local_speeds = grid_speeds(
        (first_plane + jnp.arange(plane_count, dtype=jnp.int32)).astype(jnp.float32)
    )
    moment_totals = lax.psum(combine_planes(partial_value, local_speeds[:, None, None]), "vz")
    cell_entries = tuple(
        (entry_array[None, :, :, None] for entry_array in cell_state(moment_totals))
    )
    grid_spacing = 2.0 * vel_max / V
    pointwise_rate = collision_rate[None, :, :, None]
    collide_rate = collision_scale * pointwise_rate
    relaxation_rate = relax_scale * pointwise_rate
    stiffness_factor = cell_entries[4] / (grid_spacing * grid_spacing)
    diagonal_factor = 1.0 + relaxation_rate + 6.0 * collide_rate * stiffness_factor
    index_y = jnp.arange(velocity_width, dtype=jnp.int32) % V
    upper_mask = (index_y < V - 1).astype(jnp.float32)
    lower_mask = (index_y > 0).astype(jnp.float32)
    vertical_speeds = local_speeds[:, None, None, None]
    forcing_term = transported + relaxation_rate * maxwellian(
        cell_entries, velocity_x_grid, velocity_y_grid, vertical_speeds
    )
    current_guess = transported
    for sweep_id in range(SWEEPS):
        bordered_grid = with_halo(current_guess, (("vz", 0),), 1, False)
        current_guess = relaxation_pass(
            bordered_grid,
            forcing_term,
            diagonal_factor,
            vertical_speeds,
            cell_entries,
            collide_rate,
            velocity_x_grid,
            velocity_y_grid,
            upper_mask,
            lower_mask,
        )
    return current_guess


def solution(mesh):
    return jax.shard_map(
        shards,
        mesh=mesh,
        in_specs=(P("vz", "space", None, None), P("space", None)),
        out_specs=P("vz", "space", None, None),
        check_vma=False,
    )
```

profile of v0, /device:TPU:1, one launch (start us, length us, event | category | flops | bytes accessed | tf_op | source)
XLA Modules:
  0.0 159.6 jit_solution(4560179693643808710)
XLA Ops:
  0.0 13.5 %collective-permute-start = (f32[12,2,8,2304]{3,2,1,0:T(8,128)}, f32[12,2,8,2304]{3,2,1,0:T(8,128)S(1)}, u32[]{:S(2)}, u32[]{:S(2)}) collective-permute-start(f32[12,2,8,2304]{3,2,1,0:T(8,128)} %param.2), channel_id=1, source_target_pairs={{4,0},{8,4},{12,8},{16,12},{20,16},{24,20},{28,24},{32,28},{36,32}... | collective-permute-start | bytes 5308424 | tf_op jit(solution)/shard_map/ppermute | solution.py:26
  13.5 1.9 %collective-permute-start.1 = (f32[12,2,8,2304]{3,2,1,0:T(8,128)}, f32[12,2,8,2304]{3,2,1,0:T(8,128)}, u32[]{:S(2)}, u32[]{:S(2)}) collective-permute-start(f32[12,2,8,2304]{3,2,1,0:T(8,128)} %param.2), channel_id=1, source_target_pairs={{0,4},{4,8},{8,12},{12,16},{16,20},{20,24},{24,28},{28,32},{32,36}... | collective-permute-start | bytes 5308424 | tf_op jit(solution)/shard_map/ppermute | solution.py:23
  15.5 0.6 broadcast_add_fusion.4
  16.1 0.6 add_multiply_fusion.1
  16.8 0.7 stack_reshape.5
  17.5 0.7 multiply_add_fusion.6
  18.3 10.0 %fusion = f32[4,12,2,8]{1,0,3,2:T(4,128)S(1)} fusion(f32[12,2,8,2304]{3,2,1,0:T(8,128)} %param.2, f32[2304,1]{0,1:T(1,128)S(1)} %multiply_add_fusion.6, f32[2304,1]{0,1:T(1,128)S(1)} %stack_tile.5, f32[2304,1]{0,1:T(1,128)} %stack_reshape.5, f32[4]{0:T(128)S(1)} %pad.24.clone), kind=kOutput, calls=%fused_computation.17 | convolution fusion | flops 21261312 | bytes 1800208 | tf_op jit(solution)/shard_map/zxyk,kw->wzxy/dot_general | solution.py:193
  28.2 0.8 slice_reduce_fusion
  29.0 0.7 reduce_sum.45
  29.7 1.2 constant_dynamic-update-slice_fusion.4
  30.9 1.3 constant_dynamic-update-slice_fusion.3
  32.2 1.3 constant_dynamic-update-slice_fusion.2
  33.4 0.8 add_reduce_fusion
  34.2 0.5 constant_dynamic-update-slice_fusion.1
  34.7 0.6 constant_dynamic-update-slice_fusion
  35.3 58.7 %psum.7 = f32[5,2,8]{2,1,0:T(2,128)S(1)} all-reduce(f32[5,2,8]{2,1,0:T(2,128)} %constant_dynamic-update-slice_fusion), channel_id=1, replica_groups=mesh['space'=128,'vz'=4] {'vz'}, use_global_device_ids=true, to_apply=%region_5.6 | all-reduce | flops 80 | bytes 640 | tf_op jit(solution)/shard_map/psum | solution.py:200
  94.0 0.6 bitcast_multiply_fusion
  94.6 1.3 broadcast_multiply_fusion.3
  95.9 0.6 copy-done.10
  96.5 1.4 multiply_add_fusion.7
  97.8 0.8 tile.38
  98.6 1.4 reshape.331
  100.1 1.4 copy.6
  101.4 1.4 copy.7
  102.8 1.4 copy.5
  104.2 0.7 broadcast_add_fusion.3
  105.0 0.9 multiply_add_fusion.4
  105.9 1.9 %multiply_add_fusion.2 = (f32[12,2,8,1152]{3,2,1,0:T(8,128)S(1)}, f32[12,2,8,1152]{3,2,1,0:T(8,128)S(1)}) fusion(f32[12,2,8,2304]{3,2,1,0:T(8,128)} %collective-permute-done.1, f32[12,2,8,2304]{3,2,1,0:T(8,128)S(1)} %copy-done, f32[1152]{0:T(1024)S(1)} %get-tuple-element.53, f32[1152]{0:T(1024)S(1)} %get-tuple-element.51, f32[1152]{0:T(1024)S(1)} %get-tuple-element.52, ...), kind=kLoop, calls=%fused_computation.53 | loop fusion | flops 5308416 | bytes 10649600 | tf_op jit(solution)/shard_map/add | solution.py:42
  109.1 2.0 %multiply_add_fusion.1 = f32[12,2,8,2304]{3,2,1,0:T(8,128)S(1)} fusion(f32[12,2,2,2304]{3,2,1,0:T(2,128)S(1)} %get-tuple-element.37, f32[12,2,6,2304]{3,2,1,0:T(8,128)S(1)} %get-tuple-element.39, f32[12,2,6,2304]{3,2,1,0:T(8,128)S(1)} %get-tuple-element.38, f32[12,2,2,2304]{3,2,1,0:T(2,128)S(1)} %get-tuple-element.36, ...), kind=kLoop, calls=%fused_computation.50 | loop fusion | flops 7962624 | bytes 10637568 | tf_op jit(solution)/shard_map/add | solution.py:42
  111.2 0.6 fusion.59
  111.8 2.1 %collective-permute-start.2 = (f32[1,2,8,2304]{3,2,1,0:T(8,128)S(1)}, f32[1,2,8,2304]{3,2,1,0:T(8,128)S(1)}, u32[]{:S(2)}, u32[]{:S(2)}) collective-permute-start(f32[1,2,8,2304]{3,2,1,0:T(8,128)S(1)} %get-tuple-element.30), channel_id=1, source_target_pairs={{1,0},{2,1},{3,2},{5,4},{6,5},{7,6},{9,8},{10,9},{11,10},{13,12},{... | collective-permute-start | bytes 442376 | tf_op jit(solution)/shard_map/ppermute | solution.py:26
  113.9 7.7 %collective-permute-start.3 = (f32[1,2,8,2304]{3,2,1,0:T(8,128)S(1)}, f32[1,2,8,2304]{3,2,1,0:T(8,128)S(1)}, u32[]{:S(2)}, u32[]{:S(2)}) collective-permute-start(f32[1,2,8,2304]{3,2,1,0:T(8,128)S(1)} %get-tuple-element.31), channel_id=1, source_target_pairs={{0,1},{1,2},{2,3},{4,5},{5,6},{6,7},{8,9},{9,10},{10,11},{12,13},{... | collective-permute-start | bytes 442376 | tf_op jit(solution)/shard_map/ppermute | solution.py:23
  121.6 0.6 fusion.58
  122.5 1.4 collective-permute-done.3
  124.0 2.1 %fusion.22 = f32[12,2,8,2304]{3,2,1,0:T(8,128)S(1)} fusion(f32[12,2,8,2304]{3,2,1,0:T(8,128)S(1)} %multiply_add_fusion.1, f32[1,2,8,2304]{3,2,1,0:T(8,128)S(1)} %collective-permute-done.3, f32[1,2,8,2304]{3,2,1,0:T(8,128)S(1)} %collective-permute-done.2, f32[12,2,8,2303]{3,2,1,0:T(8,128)S(1)} %get-tuple-element.29, ...), kind=kLoop, calls=%fused_computation.44 | loop fusion | flops 10616832 | bytes 11576384 | tf_op jit(solution)/shard_map/div | solution.py:161
  126.1 0.6 fusion.56
  126.7 1.9 %collective-permute-start.4 = (f32[1,2,8,2304]{3,2,1,0:T(8,128)S(1)}, f32[1,2,8,2304]{3,2,1,0:T(8,128)S(1)}, u32[]{:S(2)}, u32[]{:S(2)}) collective-permute-start(f32[1,2,8,2304]{3,2,1,0:T(8,128)S(1)} %get-tuple-element.24), channel_id=1, source_target_pairs={{1,0},{2,1},{3,2},{5,4},{6,5},{7,6},{9,8},{10,9},{11,10},{13,12},{... | collective-permute-start | bytes 442376 | tf_op jit(solution)/shard_map/ppermute | solution.py:26
  128.6 8.6 %collective-permute-start.5 = (f32[1,2,8,2304]{3,2,1,0:T(8,128)S(1)}, f32[1,2,8,2304]{3,2,1,0:T(8,128)S(1)}, u32[]{:S(2)}, u32[]{:S(2)}) collective-permute-start(f32[1,2,8,2304]{3,2,1,0:T(8,128)S(1)} %get-tuple-element.25), channel_id=1, source_target_pairs={{0,1},{1,2},{2,3},{4,5},{5,6},{6,7},{8,9},{9,10},{10,11},{12,13},{... | collective-permute-start | bytes 442376 | tf_op jit(solution)/shard_map/ppermute | solution.py:23
  137.2 0.6 fusion.55
  138.0 2.3 %collective-permute-done.5 = f32[1,2,8,2304]{3,2,1,0:T(8,128)S(1)} collective-permute-done((f32[1,2,8,2304]{3,2,1,0:T(8,128)S(1)}, f32[1,2,8,2304]{3,2,1,0:T(8,128)S(1)}, u32[]{:S(2)}, u32[]{:S(2)}) %collective-permute-start.5) | collective-permute-done | bytes 147488 | tf_op jit(solution)/shard_map/ppermute | solution.py:23
  140.3 2.0 %fusion.16 = f32[12,2,8,2304]{3,2,1,0:T(8,128)S(1)} fusion(f32[12,2,8,2304]{3,2,1,0:T(8,128)S(1)} %fusion.22, f32[1,2,8,2304]{3,2,1,0:T(8,128)S(1)} %collective-permute-done.5, f32[1,2,8,2304]{3,2,1,0:T(8,128)S(1)} %collective-permute-done.4, f32[12,2,8,2303]{3,2,1,0:T(8,128)S(1)} %get-tuple-element.23, f32[12,2,8,2303]{3,2,1,0:T(8,128)S(1)} %get-tuple-element.22, ...), kind=kLoop, calls=%fused_computation.36 | loop fusion | flops 10616832 | bytes 13345856 | tf_op jit(solution)/shard_map/div | solution.py:161
  142.4 0.6 fusion.53
  143.0 1.9 %collective-permute-start.6 = (f32[1,2,8,2304]{3,2,1,0:T(8,128)S(1)}, f32[1,2,8,2304]{3,2,1,0:T(8,128)S(1)}, u32[]{:S(2)}, u32[]{:S(2)}) collective-permute-start(f32[1,2,8,2304]{3,2,1,0:T(8,128)S(1)} %get-tuple-element.18), channel_id=1, source_target_pairs={{1,0},{2,1},{3,2},{5,4},{6,5},{7,6},{9,8},{10,9},{11,10},{13,12},{... | collective-permute-start | bytes 442376 | tf_op jit(solution)/shard_map/ppermute | solution.py:26
  145.0 8.4 %collective-permute-start.7 = (f32[1,2,8,2304]{3,2,1,0:T(8,128)S(1)}, f32[1,2,8,2304]{3,2,1,0:T(8,128)S(1)}, u32[]{:S(2)}, u32[]{:S(2)}) collective-permute-start(f32[1,2,8,2304]{3,2,1,0:T(8,128)S(1)} %get-tuple-element.19), channel_id=1, source_target_pairs={{0,1},{1,2},{2,3},{4,5},{5,6},{6,7},{8,9},{9,10},{10,11},{12,13},{... | collective-permute-start | bytes 442376 | tf_op jit(solution)/shard_map/ppermute | solution.py:23
  153.4 0.6 fusion.52
  154.0 0.4 collective-permute-done.6
  154.3 2.3 %collective-permute-done.7 = f32[1,2,8,2304]{3,2,1,0:T(8,128)S(1)} collective-permute-done((f32[1,2,8,2304]{3,2,1,0:T(8,128)S(1)}, f32[1,2,8,2304]{3,2,1,0:T(8,128)S(1)}, u32[]{:S(2)}, u32[]{:S(2)}) %collective-permute-start.7) | collective-permute-done | bytes 147488 | tf_op jit(solution)/shard_map/ppermute | solution.py:23
  156.7 2.9 %fusion.10 = f32[12,2,8,2304]{3,2,1,0:T(8,128)} fusion(f32[12,2,8,2304]{3,2,1,0:T(8,128)S(1)} %fusion.16, f32[1,2,8,2304]{3,2,1,0:T(8,128)S(1)} %collective-permute-done.7, f32[1,2,8,2304]{3,2,1,0:T(8,128)S(1)} %collective-permute-done.6, f32[12,2,8,2303]{3,2,1,0:T(8,128)S(1)} %get-tuple-element.17, f32[12,2,8,2303]{3,2,1,0:T(8,128)S(1)} %get-tuple-element.16, ...), kind=kLoop, calls=%fused_computation.28 | loop fusion | flops 10616832 | bytes 13345856 | tf_op jit(solution)/shard_map/div | solution.py:161
  (41 shorter events, 2.1 us)
Async XLA Ops:
  0.0 105.8 %collective-permute-start = (f32[12,2,8,2304]{3,2,1,0:T(8,128)}, f32[12,2,8,2304]{3,2,1,0:T(8,128)S(1)}, u32[]{:S(2)}, u32[]{:S(2)}) collective-permute-start(f32[12,2,8,2304]{3,2,1,0:T(8,128)} %param.2), channel_id=1, source_target_pairs={{4,0},{8,4},{12,8},{16,12},{20,16},{24,20},{28,24},{32,28},{36,32}... | collective-permute-start | bytes 5308424 | tf_op jit(solution)/shard_map/ppermute | solution.py:26
  13.5 92.3 %collective-permute-start.1 = (f32[12,2,8,2304]{3,2,1,0:T(8,128)}, f32[12,2,8,2304]{3,2,1,0:T(8,128)}, u32[]{:S(2)}, u32[]{:S(2)}) collective-permute-start(f32[12,2,8,2304]{3,2,1,0:T(8,128)} %param.2), channel_id=1, source_target_pairs={{0,4},{4,8},{8,12},{12,16},{16,20},{20,24},{24,28},{28,32},{32,36}... | collective-permute-start | bytes 5308424 | tf_op jit(solution)/shard_map/ppermute | solution.py:23
  16.7 0.9 copy-start.1
  16.8 0.7 copy-start.2
  18.3 87.6 %copy-start = (f32[12,2,8,2304]{3,2,1,0:T(8,128)S(1)}, f32[12,2,8,2304]{3,2,1,0:T(8,128)}, u32[]{:S(2)}) copy-start(f32[12,2,8,2304]{3,2,1,0:T(8,128)} %param.2) | copy-start | bytes 5308420
  95.9 0.6 copy-start.10
  111.8 10.8 %collective-permute-start.2 = (f32[1,2,8,2304]{3,2,1,0:T(8,128)S(1)}, f32[1,2,8,2304]{3,2,1,0:T(8,128)S(1)}, u32[]{:S(2)}, u32[]{:S(2)}) collective-permute-start(f32[1,2,8,2304]{3,2,1,0:T(8,128)S(1)} %get-tuple-element.30), channel_id=1, source_target_pairs={{1,0},{2,1},{3,2},{5,4},{6,5},{7,6},{9,8},{10,9},{11,10},{13,12},{... | collective-permute-start | bytes 442376 | tf_op jit(solution)/shard_map/ppermute | solution.py:26
  113.8 10.1 %copy-start.3 = (f32[12,2,8]{2,1,0:T(2,128)S(1)}, f32[12,2,8]{2,1,0:T(2,128)}, u32[]{:S(2)}) copy-start(f32[12,2,8]{2,1,0:T(2,128)} %copy.6) | copy-start | bytes 2308
  113.8 10.1 %copy-start.4 = (f32[12,2,8]{2,1,0:T(2,128)S(1)}, f32[12,2,8]{2,1,0:T(2,128)}, u32[]{:S(2)}) copy-start(f32[12,2,8]{2,1,0:T(2,128)} %copy.7) | copy-start | bytes 2308
  113.9 10.1 %copy-start.5 = (f32[12,2,8]{2,1,0:T(2,128)S(1)}, f32[12,2,8]{2,1,0:T(2,128)}, u32[]{:S(2)}) copy-start(f32[12,2,8]{2,1,0:T(2,128)} %copy.5) | copy-start | bytes 2308
  113.9 10.1 %copy-start.6 = (f32[2,8]{1,0:T(2,128)S(1)}, f32[2,8]{1,0:T(2,128)}, u32[]{:S(2)}) copy-start(f32[2,8]{1,0:T(2,128)} %get-tuple-element.61) | copy-start | bytes 196
  113.9 10.1 %copy-start.7 = (f32[2,8]{1,0:T(2,128)S(1)}, f32[2,8]{1,0:T(2,128)}, u32[]{:S(2)}) copy-start(f32[2,8]{1,0:T(2,128)} %get-tuple-element.62) | copy-start | bytes 196
  113.9 10.1 %copy-start.8 = (f32[2,8]{1,0:T(2,128)S(1)}, f32[2,8]{1,0:T(2,128)}, u32[]{:S(2)}) copy-start(f32[2,8]{1,0:T(2,128)} %get-tuple-element.63) | copy-start | bytes 196
  113.9 10.1 %copy-start.9 = (f32[2,8]{1,0:T(2,128)S(1)}, f32[2,8]{1,0:T(2,128)}, u32[]{:S(2)}) copy-start(f32[2,8]{1,0:T(2,128)} %get-tuple-element.65) | copy-start | bytes 196
  113.9 10.0 %collective-permute-start.3 = (f32[1,2,8,2304]{3,2,1,0:T(8,128)S(1)}, f32[1,2,8,2304]{3,2,1,0:T(8,128)S(1)}, u32[]{:S(2)}, u32[]{:S(2)}) collective-permute-start(f32[1,2,8,2304]{3,2,1,0:T(8,128)S(1)} %get-tuple-element.31), channel_id=1, source_target_pairs={{0,1},{1,2},{2,3},{4,5},{5,6},{6,7},{8,9},{9,10},{10,11},{12,13},{... | collective-permute-start | bytes 442376 | tf_op jit(solution)/shard_map/ppermute | solution.py:23
  126.7 11.3 %collective-permute-start.4 = (f32[1,2,8,2304]{3,2,1,0:T(8,128)S(1)}, f32[1,2,8,2304]{3,2,1,0:T(8,128)S(1)}, u32[]{:S(2)}, u32[]{:S(2)}) collective-permute-start(f32[1,2,8,2304]{3,2,1,0:T(8,128)S(1)} %get-tuple-element.24), channel_id=1, source_target_pairs={{1,0},{2,1},{3,2},{5,4},{6,5},{7,6},{9,8},{10,9},{11,10},{13,12},{... | collective-permute-start | bytes 442376 | tf_op jit(solution)/shard_map/ppermute | solution.py:26
  128.6 11.7 %collective-permute-start.5 = (f32[1,2,8,2304]{3,2,1,0:T(8,128)S(1)}, f32[1,2,8,2304]{3,2,1,0:T(8,128)S(1)}, u32[]{:S(2)}, u32[]{:S(2)}) collective-permute-start(f32[1,2,8,2304]{3,2,1,0:T(8,128)S(1)} %get-tuple-element.25), channel_id=1, source_target_pairs={{0,1},{1,2},{2,3},{4,5},{5,6},{6,7},{8,9},{9,10},{10,11},{12,13},{... | collective-permute-start | bytes 442376 | tf_op jit(solution)/shard_map/ppermute | solution.py:23
  143.0 11.3 %collective-permute-start.6 = (f32[1,2,8,2304]{3,2,1,0:T(8,128)S(1)}, f32[1,2,8,2304]{3,2,1,0:T(8,128)S(1)}, u32[]{:S(2)}, u32[]{:S(2)}) collective-permute-start(f32[1,2,8,2304]{3,2,1,0:T(8,128)S(1)} %get-tuple-element.18), channel_id=1, source_target_pairs={{1,0},{2,1},{3,2},{5,4},{6,5},{7,6},{9,8},{10,9},{11,10},{13,12},{... | collective-permute-start | bytes 442376 | tf_op jit(solution)/shard_map/ppermute | solution.py:26
  145.0 11.7 %collective-permute-start.7 = (f32[1,2,8,2304]{3,2,1,0:T(8,128)S(1)}, f32[1,2,8,2304]{3,2,1,0:T(8,128)S(1)}, u32[]{:S(2)}, u32[]{:S(2)}) collective-permute-start(f32[1,2,8,2304]{3,2,1,0:T(8,128)S(1)} %get-tuple-element.19), channel_id=1, source_target_pairs={{0,1},{1,2},{2,3},{4,5},{5,6},{6,7},{8,9},{9,10},{10,11},{12,13},{... | collective-permute-start | bytes 442376 | tf_op jit(solution)/shard_map/ppermute | solution.py:23
where the time goes:
time: 160 us
  blocking collectives  58.7 us (37%)
  starting transfers between devices  46 us (29%)
  other arithmetic  21.2 us (13%)
  local copies, waits for them, and re-layouts  16.4 us (10%)
  matrix products  9.96 us (6%)
  waiting for transfers between devices  6.96 us (4%)
    psum x1, blocking collectives, shards(): lax.psum(combine_planes(partial_value, local_speeds[:, None, None]), 'vz')  58.7 us
    ppermute x4, starting transfers between devices, with_halo(): lax.ppermute(lax.slice_in_dim(block, block.shape[dim] - width, None, axis...  26.6 us
    ppermute x4, starting transfers between devices, with_halo(): lax.ppermute(lax.slice_in_dim(block, 0, width, axis=dim), axis, backward)  19.4 us
    dot_general x1, matrix products, shards(): jnp.einsum('zxyk,kw->wzxy', distribution, weights, precision=lax.Precisio...  9.96 us
    div x3, other arithmetic, relaxation_pass(): return running_total / diagonal_factor  7.02 us
    ppermute x4, waiting for transfers between devices, with_halo(): lax.ppermute(lax.slice_in_dim(block, block.shape[dim] - width, None, axis...  6.09 us
    unnamed x26, local copies, waits for them, and re-layouts  4.9 us
    add x2, other arithmetic, beam_warming(): middle - 0.5 * magnitude * (3.0 * middle - 4.0 * near_cells + far_cells)  3.96 us
  transfers between devices with their start and end apart: 8, of which 6 were waited for; matrix products, arithmetic and copies ran while one was open for 21% of the time, Pallas kernels for 0%

commit v1 on v0

v1 whole, which is shorter than its diff:
```python
import functools
import math

import jax
import jax.numpy as jnp
from jax import lax
from jax.experimental import pallas as pl
from jax.experimental.pallas import tpu as pltpu
from jax.sharding import PartitionSpec as P

V = 48
WIDTH = V * V
HALF = WIDTH // 2
DEPTH = 3

vel_max = 4.5
step_ratio = 0.1
collision_scale = 0.004
relax_scale = 0.5
spacing = 2.0 * vel_max / V

VMEM_LIMIT = 40 * 1024 * 1024


def speed_of(position):
    return vel_max * (2.0 * position - (V - 1.0)) / V


def lane_grid(first, width, rows=8):
    lane = lax.broadcasted_iota(jnp.int32, (rows, width), 1).astype(jnp.float32) + float(first)
    column = jnp.floor((lane + 0.5) * (1.0 / V))
    return column, lane - V * column


def wide(tile):
    return jnp.concatenate([tile] * (WIDTH // 128), axis=1)


def moments_kernel(slab_ref, f_ref, out_ref):
    planes, columns = f_ref.shape[0], f_ref.shape[1]
    slab = slab_ref[0]
    chunk = 768
    lane = lax.broadcasted_iota(jnp.int32, (8, 128), 1)
    for column in range(columns):
        totals = [jnp.zeros((8, 1), jnp.float32)] * 5
        for first in range(0, WIDTH, chunk):
            mass = jnp.zeros((8, chunk), jnp.float32)
            flow = jnp.zeros((8, chunk), jnp.float32)
            heat = jnp.zeros((8, chunk), jnp.float32)
            for plane in range(planes):
                cz = speed_of((slab * planes + plane).astype(jnp.float32))
                f = f_ref[plane, column, :, first : first + chunk]
                scaled = f * cz
                mass += f
                flow += scaled
                heat += scaled * cz
            vx, vy = lane_grid(first, chunk)
            cx, cy = speed_of(vx), speed_of(vy)
            parts = (mass, mass * cx, mass * cy, flow, mass * (cx * cx + cy * cy) + heat)
            totals = [t + jnp.sum(p, axis=1, keepdims=True) for t, p in zip(totals, parts)]
        row = jnp.zeros((8, 128), jnp.float32)
        for k in range(5):
            row = jnp.where(lane == k, totals[k], row)
        out_ref[column] = row


def coefficients_kernel(total_ref, rate_ref, coef_ref, cell_ref):
    for column in range(total_ref.shape[0]):
        m0, m1, m2, m3, m4 = (
            jnp.broadcast_to(total_ref[column, :, k : k + 1], (8, 128)) for k in range(5)
        )
        rate = rate_ref[column]
        density = m0 * spacing**3
        ux, uy, uz = m1 / m0, m2 / m0, m3 / m0
        temperature = (m4 / m0 - ux * ux - uy * uy - uz * uz) / 3.0
        stiff = temperature / (spacing * spacing)
        collide, relax = collision_scale * rate, relax_scale * rate
        inverse = 1.0 / (1.0 + relax + 6.0 * collide * stiff)
        middle = collide * inverse * (stiff + 0.5)
        slope = collide * inverse * (0.5 / spacing)
        root = 1.0 / jnp.sqrt(2.0 * math.pi * temperature)
        scale = density * (root * root * root) * (relax * inverse)
        for k, value in enumerate((middle, slope, uz, temperature, inverse)):
            cell_ref[column, k] = value
        vx, vy = lane_grid(0, WIDTH)
        dx, dy = speed_of(vx) - wide(ux), speed_of(vy) - wide(uy)
        middle, slope = wide(middle), wide(slope)
        coef_ref[column, 0] = jnp.where(vx < V - 1.5, middle + slope * dx, 0.0)
        coef_ref[column, 1] = jnp.where(vx > 0.5, middle - slope * dx, 0.0)
        coef_ref[column, 2] = jnp.where(vy < V - 1.5, middle + slope * dy, 0.0)
        coef_ref[column, 3] = jnp.where(vy > 0.5, middle - slope * dy, 0.0)
        coef_ref[column, 4] = wide(scale) * jnp.exp(
            -(dx * dx + dy * dy) / (2.0 * wide(temperature))
        )


def upwind_weights(speed):
    a = step_ratio * jnp.abs(speed)
    return 1.0 - 1.5 * a + 0.5 * a * a, 2.0 * a - a * a, 0.5 * a * a - 0.5 * a


def fill_weights(weight_ref):
    vx, vy = lane_grid(0, WIDTH)
    for k, value in enumerate(upwind_weights(speed_of(vx)) + upwind_weights(speed_of(vy))):
        weight_ref[k] = value
    weight_ref[6] = jnp.where(vy > V // 2 - 0.5, 1.0, 0.0)


def transport_plane(f_ref, plane, low_ref, high_ref, entry, weight_ref, store):
    for column in range(2):
        for part in range(2):
            lanes = pl.ds(part * HALF, HALF)
            f = f_ref[plane, column, :, lanes]
            if part == 1:
                near = low_ref[entry, 1] if column == 0 else f_ref[plane, 0, :, lanes]
                far = low_ref[entry, column]
            else:
                near = f_ref[plane, 1, :, lanes] if column == 0 else high_ref[entry, 0]
                far = high_ref[entry, column]
            swept = (
                weight_ref[0, :, lanes] * f
                + weight_ref[1, :, lanes] * near
                + weight_ref[2, :, lanes] * far
            )
            positive = weight_ref[6, :, lanes] > 0.5
            near = jnp.where(positive, pltpu.roll(swept, 1, 0), pltpu.roll(swept, 7, 0))
            far = jnp.where(positive, pltpu.roll(swept, 2, 0), pltpu.roll(swept, 6, 0))
            store(
                column,
                lanes,
                weight_ref[3, :, lanes] * swept
                + weight_ref[4, :, lanes] * near
                + weight_ref[5, :, lanes] * far,
            )


def edges_kernel(slab_ref, f_ref, low_ref, high_ref, outer_ref, inner_ref, weight_ref):
    planes = f_ref.shape[0]
    odd = lax.rem(slab_ref[0], 2)
    fill_weights(weight_ref)
    for side, target in ((0, outer_ref), (1, inner_ref)):

        def step(k, carry, side=side, target=target):
            place = k + side * DEPTH
            entry = jnp.where(odd == 1, 2 * DEPTH - 1 - place, place)
            plane = jnp.where(entry < DEPTH, entry, entry + planes - 2 * DEPTH)

            def store(column, lanes, value):
                target[k, column, :, lanes] = value

            transport_plane(f_ref, plane, low_ref, high_ref, entry, weight_ref, store)
            return carry

        lax.fori_loop(0, DEPTH, step, 0)


def plane_speed(slab, odd, planes, place):
    position = slab * planes + jnp.where(odd == 1, planes - 1 - place, place)
    return speed_of(position.astype(jnp.float32))


def source_row(guess, coef_ref, cell_ref, column, cz):
    distance = cz - cell_ref[column, 2]
    fall = jnp.exp(-(distance * distance) / (2.0 * cell_ref[column, 3]))
    return wide(cell_ref[column, 4]) * guess + wide(fall) * coef_ref[column, 4]


def sweep_row(source, guess, after, before, coef_ref, cell_ref, column, cz, sign):
    tilt = sign * cell_ref[column, 1] * (cz - cell_ref[column, 2])
    middle = cell_ref[column, 0]
    total = source + wide(middle + tilt) * after + wide(middle - tilt) * before
    total += coef_ref[column, 0] * pltpu.roll(guess, WIDTH - V, 1)
    total += coef_ref[column, 1] * pltpu.roll(guess, V, 1)
    total += coef_ref[column, 2] * pltpu.roll(guess, WIDTH - 1, 1)
    total += coef_ref[column, 3] * pltpu.roll(guess, 1, 1)
    return total


def main_kernel(
    slab_ref, f_ref, low_ref, high_ref, outer_ref, inner_ref, halo_ref, coef_ref, cell_ref,
    out_ref, kept_ref, weight_ref, zero_ref, source_ref, one_ref, two_ref,
):
    planes = f_ref.shape[0]
    slab = slab_ref[0]
    odd = lax.rem(slab, 2)
    sign = jnp.where(odd == 1, -1.0, 1.0)
    fill_weights(weight_ref)
    for k in range(DEPTH):
        zero_ref[k] = outer_ref[k]
        zero_ref[planes - DEPTH + k] = inner_ref[k]
        zero_ref[planes + k] = halo_ref[DEPTH - 1 - k]

    def transport_step(k, carry):
        place = DEPTH + k
        plane = jnp.where(odd == 1, planes - 1 - place, place)

        def store(column, lanes, value):
            zero_ref[place, column, :, lanes] = value

        transport_plane(f_ref, plane, low_ref, high_ref, plane - DEPTH, weight_ref, store)
        return carry

    lax.fori_loop(0, planes - 2 * DEPTH, transport_step, 0)

    def source_step(place, carry):
        cz = plane_speed(slab, odd, planes, place)
        for column in range(2):
            source_ref[place, column] = source_row(
                zero_ref[place, column], coef_ref, cell_ref, column, cz
            )
        return carry

    lax.fori_loop(0, planes + DEPTH - 1, source_step, 0)

    def sweep(old, new, first, last, flip=False):
        def step(place, carry):
            cz = plane_speed(slab, odd, planes, place)
            spot = jnp.where(odd == 1, planes - 1 - place, place) if flip else place
            for column in range(2):
                new[spot, column] = sweep_row(
                    source_ref[place, column], old[place, column], old[place + 1, column],
                    old[place - 1, column], coef_ref, cell_ref, column, cz, sign,
                )
            return carry

        lax.fori_loop(first, last, step, 0)

    sweep(zero_ref, one_ref, 1, planes + 2)
    sweep(one_ref, two_ref, 2, planes + 1)
    sweep(two_ref, out_ref, 3, planes, flip=True)
    for k, (ref, place) in enumerate(
        ((source_ref, 0), (source_ref, 1), (source_ref, 2), (one_ref, 1), (one_ref, 2), (two_ref, 2), (two_ref, 3))
    ):
        kept_ref[k] = ref[place]


def last_kernel(
    slab_ref, halo_ref, outer_ref, kept_ref, coef_ref, cell_ref, before_ref, out_ref,
    zero_ref, source_ref, one_ref, two_ref,
):
    planes = slab_ref[1]
    slab = slab_ref[0]
    odd = lax.rem(slab, 2)
    sign = jnp.where(odd == 1, -1.0, 1.0)
    inside = jnp.where((slab == 0) | (slab == slab_ref[2] - 1), 0.0, 1.0)
    for k in range(DEPTH):
        zero_ref[k] = halo_ref[DEPTH - 1 - k]
        source_ref[DEPTH + k] = kept_ref[k]
    for k in range(2):
        zero_ref[DEPTH + k] = outer_ref[k]
        one_ref[DEPTH + 1 + k] = kept_ref[3 + k]
        two_ref[DEPTH + 2 + k] = kept_ref[5 + k]

    for place in (-2, -1):
        cz = plane_speed(slab, odd, planes, place)
        for column in range(2):
            source_ref[place + 3, column] = source_row(
                zero_ref[place + 3, column], coef_ref, cell_ref, column, cz
            )

    def sweep(old, new, first, flip=False):
        def step(k, carry):
            place = first + k
            cz = plane_speed(slab, odd, planes, place)
            gain = jnp.where(place < 0, inside, 1.0)
            spot = jnp.where(odd == 1, DEPTH - 1 - place, place) if flip else place + 3
            for column in range(2):
                new[spot, column] = gain * sweep_row(
                    source_ref[place + 3, column], old[place + 3, column], old[place + 4, column],
                    old[place + 2, column], coef_ref, cell_ref, column, cz, sign,
                )
            return carry

        lax.fori_loop(0, DEPTH, step, 0)

    sweep(zero_ref, one_ref, -2)
    sweep(one_ref, two_ref, -1)
    sweep(two_ref, out_ref, 0, flip=True)


def shape(*dims):
    return jax.ShapeDtypeStruct(dims, jnp.float32)


PARAMS = pltpu.CompilerParams(vmem_limit_bytes=VMEM_LIMIT)
SMEM = pl.BlockSpec(memory_space=pltpu.SMEM)
VMEM = pl.BlockSpec(memory_space=pltpu.VMEM)


def shards(distribution, collision_rate):
    planes, columns, rows, width = distribution.shape
    spaces, slabs = lax.axis_size("space"), lax.axis_size("vz")
    slab = lax.axis_index("vz").astype(jnp.int32)
    facts = jnp.stack([slab, jnp.int32(planes), jnp.int32(slabs)])

    forward = [(i, (i + 1) % spaces) for i in range(spaces)]
    backward = [(b, a) for a, b in forward]
    partners = [(i, i ^ 1) for i in range(slabs)]
    crossing = [(i, i + 1) for i in range(1, slabs - 1, 2)]
    crossing += [(b, a) for a, b in crossing]
    opposite = [(i, slabs - 1 - i) for i in range(slabs)]

    def both_ways(block):
        return (
            lax.ppermute(block[..., HALF:], "space", forward),
            lax.ppermute(block[..., :HALF], "space", backward),
        )

    edges = jnp.concatenate([distribution[:DEPTH], distribution[planes - DEPTH :]], axis=0)
    edge_low, edge_high = both_ways(edges)
    low, high = both_ways(distribution[DEPTH : planes - DEPTH])

    part = pl.pallas_call(
        moments_kernel,
        out_shape=shape(columns, rows, 128),
        in_specs=[SMEM, VMEM],
        out_specs=VMEM,
        compiler_params=PARAMS,
    )(facts, distribution)
    part = part + lax.ppermute(part, "vz", partners)
    total = part + lax.ppermute(part, "vz", opposite)

    outer, inner = pl.pallas_call(
        edges_kernel,
        out_shape=[shape(DEPTH, columns, rows, width)] * 2,
        in_specs=[SMEM, VMEM, VMEM, VMEM],
        out_specs=[VMEM, VMEM],
        scratch_shapes=[pltpu.VMEM((7, rows, width), jnp.float32)],
        compiler_params=PARAMS,
    )(facts, distribution, edge_low, edge_high)
    outer_halo = lax.ppermute(outer, "vz", crossing)
    inner_halo = lax.ppermute(inner, "vz", partners)

    coef, cell = pl.pallas_call(
        coefficients_kernel,
        out_shape=[shape(columns, 5, rows, width), shape(columns, 5, rows, 128)],
        in_specs=[VMEM, VMEM],
        out_specs=[VMEM, VMEM],
        compiler_params=PARAMS,
    )(total, jnp.broadcast_to(collision_rate[:, :, None], (columns, rows, 128)))

    block = (columns, rows, width)
    most, kept = pl.pallas_call(
        main_kernel,
        out_shape=[shape(planes, *block), shape(7, *block)],
        in_specs=[SMEM] + [VMEM] * 8,
        out_specs=[VMEM, VMEM],
        scratch_shapes=[
            pltpu.VMEM((7, rows, width), jnp.float32),
            pltpu.VMEM((planes + DEPTH, *block), jnp.float32),
            pltpu.VMEM((planes + DEPTH, *block), jnp.float32),
            pltpu.VMEM((planes + DEPTH, *block), jnp.float32),
            pltpu.VMEM((planes + DEPTH, *block), jnp.float32),
        ],
        compiler_params=PARAMS,
    )(facts, distribution, low, high, outer, inner, inner_halo, coef, cell)

    def whole(*dims):
        return pl.BlockSpec(dims, lambda i, facts: (0,) * len(dims))

    return pl.pallas_call(
        last_kernel,
        out_shape=shape(planes, *block),
        grid_spec=pltpu.PrefetchScalarGridSpec(
            num_scalar_prefetch=1,
            grid=(1,),
            in_specs=[
                whole(DEPTH, *block),
                whole(DEPTH, *block),
                whole(7, *block),
                whole(columns, 5, rows, width),
                whole(columns, 5, rows, 128),
                pl.BlockSpec(memory_space=pl.ANY),
            ],
            out_specs=pl.BlockSpec(
                (DEPTH, *block),
                lambda i, facts: (lax.rem(facts[0], 2) * (planes // DEPTH - 1), 0, 0, 0),
            ),
            scratch_shapes=[pltpu.VMEM((8, *block), jnp.float32)] * 4,
        ),
        input_output_aliases={6: 0},
        compiler_params=PARAMS,
    )(facts, outer_halo, outer, kept, coef, cell, most)


def solution(mesh):
    return jax.shard_map(
        shards,
        mesh=mesh,
        in_specs=(P("vz", "space", None, None), P("space", None)),
        out_specs=P("vz", "space", None, None),
        check_vma=False,
    )
```

time: 160 us -> 83.6 us (0.52)
  blocking collectives: 58.7 us -> 0 us
  other arithmetic: 21.2 us -> 1.05 us
  Pallas kernels: 0 us -> 16.6 us
  local copies, waits for them, and re-layouts: 16.4 us -> 2.4 us
  waiting for transfers between devices: 6.96 us -> 17 us
  matrix products: 9.96 us -> 0 us
    psum x1 -> x0, blocking collectives: 58.7 us -> none  [shards(): lax.psum(combine_planes(partial_value, local_speeds[:, None, None]), 'vz')]
    pallas_call x0 -> x5, Pallas kernels: none -> 16.6 us  [the longest x1 10.6 us: shards(): pl.pallas_call(main_kernel, out_shape=[shape(planes, *block), shape(7, *b...]
    ppermute x8, waiting for transfers between devices: 6.96 us -> 17 us  [the longest x2 8.11 us: both_ways(): lax.ppermute(block[..., :HALF], 'space', backward)]
    dot_general x1 -> x0, matrix products: 9.96 us -> none  [shards(): jnp.einsum('zxyk,kw->wzxy', distribution, weights, precision=lax.Precisio...]
    add x7 -> x2, other arithmetic: 7.63 us -> 0.01 us  [the longest x1 0.01 us: shards(): part = part + lax.ppermute(part, 'vz', partners)]
    div x5 -> x0, other arithmetic: 7.62 us -> none  [the longest x3 7.02 us: relaxation_pass(): return running_total / diagonal_factor]
    unnamed x26 -> x4, local copies, waits for them, and re-layouts: 4.9 us -> 0.01 us
    reduce_sum x3 -> x0, other arithmetic: 2.19 us -> none  [the longest x1 0.76 us: combine_planes(): jnp.sum(partial_value[3] + vertical_speeds * vertical_speeds * zero_momen...]
  transfers between devices with their start and end apart: 8 -> 8, of which waited for: 6 -> 3; matrix products, arithmetic and copies ran while one was open for 21% -> 1% of each run, Pallas kernels for 0% -> 16%
where the time goes in v1:
time: 83.6 us; the launch traced here: 83.3 us
  starting transfers between devices  46.1 us (55%)
  waiting for transfers between devices  17 us (20%)
  Pallas kernels  16.6 us (20%)
  local copies, waits for them, and re-layouts  2.4 us (3%)
  other arithmetic  1.05 us (1%)
    ppermute x2, starting transfers between devices, both_ways(): lax.ppermute(block[..., :HALF], 'space', backward)  20 us
    pallas_call x1, Pallas kernels, shards(): pl.pallas_call(main_kernel, out_shape=[shape(planes, *block), shape(7, *b...  10.6 us
    ppermute x2, waiting for transfers between devices, both_ways(): lax.ppermute(block[..., :HALF], 'space', backward)  8.11 us
    ppermute x1, starting transfers between devices, shards(): inner_halo = lax.ppermute(inner, 'vz', partners)  7.81 us
    ppermute x1, waiting for transfers between devices, shards(): total = part + lax.ppermute(part, 'vz', opposite)  7.75 us
    ppermute x1, starting transfers between devices, shards(): outer_halo = lax.ppermute(outer, 'vz', crossing)  7.71 us
    ppermute x2, starting transfers between devices, both_ways(): lax.ppermute(block[..., HALF:], 'space', forward)  6.73 us
    pallas_call x1, Pallas kernels, shards(): pl.pallas_call(last_kernel, out_shape=shape(planes, *block), grid_spec=pl...  3.57 us
  transfers between devices with their start and end apart: 8, of which 3 were waited for; matrix products, arithmetic and copies ran while one was open for 1% of the time, Pallas kernels for 16%

profile of v1, /device:TPU:1, one launch (start us, length us, event | category | flops | bytes accessed | tf_op | source)
XLA Modules:
  0.0 83.3 jit_solution(1733151995966334921)
XLA Ops:
  0.0 0.0 copy-start
  0.0 1.3 %fusion.2 = (f32[3,2,8,2304]{3,2,1,0:T(8,128)S(1)}, f32[3,2,8,2304]{3,2,1,0:T(8,128)S(1)}) fusion(f32[12,2,8,2304]{3,2,1,0:T(8,128)} %f_ref.5), kind=kLoop, calls=%fused_computation.6 | loop fusion | bytes 1769472 | tf_op jit(solution)/shard_map/slice | solution.py:309
  1.3 1.0 %pad_maximum_fusion = (f32[6,2,8,1152]{3,2,1,0:T(8,128)}, f32[6,2,8,1152]{3,2,1,0:T(8,128)}) fusion(f32[3,2,8,2304]{3,2,1,0:T(8,128)S(1)} %get-tuple-element.19, f32[3,2,8,2304]{3,2,1,0:T(8,128)S(1)} %get-tuple-element.20), kind=kLoop, calls=%fused_computation.3 | loop fusion | flops 221184 | bytes 1769472 | tf_op jit(solution)/shard_map/concatenate | solution.py:309
  2.3 4.8 %collective-permute-start = (f32[6,2,8,1152]{3,2,1,0:T(8,128)}, f32[6,2,8,1152]{3,2,1,0:T(8,128)S(1)}, u32[]{:S(2)}, u32[]{:S(2)}) collective-permute-start(f32[6,2,8,1152]{3,2,1,0:T(8,128)} %get-tuple-element.22), channel_id=1, source_target_pairs={{0,4},{4,8},{8,12},{12,16},{16,20},{20,24},{24,28},{28,32},{32,36}... | collective-permute-start | bytes 1327112 | tf_op jit(solution)/shard_map/ppermute | solution.py:305
  7.1 10.6 %collective-permute-start.1 = (f32[6,2,8,1152]{3,2,1,0:T(8,128)}, f32[6,2,8,1152]{3,2,1,0:T(8,128)S(1)}, u32[]{:S(2)}, u32[]{:S(2)}) collective-permute-start(f32[6,2,8,1152]{3,2,1,0:T(8,128)} %get-tuple-element.21), channel_id=1, source_target_pairs={{4,0},{8,4},{12,8},{16,12},{20,16},{24,20},{28,24},{32,28},{36,32}... | collective-permute-start | bytes 1327112 | tf_op jit(solution)/shard_map/ppermute | solution.py:306
  17.8 0.0 copy-done
  17.8 1.0 %fusion.1 = (f32[6,2,8,1152]{3,2,1,0:T(8,128)}, f32[6,2,8,1152]{3,2,1,0:T(8,128)}) fusion(f32[12,2,8,2304]{3,2,1,0:T(8,128)S(1)} %copy-done), kind=kLoop, calls=%fused_computation.5 | loop fusion | bytes 1769472 | tf_op jit(solution)/shard_map/slice | solution.py:306
  18.8 1.9 %collective-permute-start.3 = (f32[6,2,8,1152]{3,2,1,0:T(8,128)}, f32[6,2,8,1152]{3,2,1,0:T(8,128)S(1)}, u32[]{:S(2)}, u32[]{:S(2)}) collective-permute-start(f32[6,2,8,1152]{3,2,1,0:T(8,128)} %get-tuple-element.18), channel_id=1, source_target_pairs={{0,4},{4,8},{8,12},{12,16},{16,20},{20,24},{24,28},{28,32},{32,36}... | collective-permute-start | bytes 1327112 | tf_op jit(solution)/shard_map/ppermute | solution.py:305
  20.7 9.4 %collective-permute-start.4 = (f32[6,2,8,1152]{3,2,1,0:T(8,128)}, f32[6,2,8,1152]{3,2,1,0:T(8,128)S(1)}, u32[]{:S(2)}, u32[]{:S(2)}) collective-permute-start(f32[6,2,8,1152]{3,2,1,0:T(8,128)} %get-tuple-element.17), channel_id=1, source_target_pairs={{4,0},{8,4},{12,8},{16,12},{20,16},{24,20},{28,24},{32,28},{36,32}... | collective-permute-start | bytes 1327112 | tf_op jit(solution)/shard_map/ppermute | solution.py:306
  30.1 0.1 pad_add_fusion.slab_ref
  30.2 0.0 copy-start.1
  30.2 0.0 collective-permute-done.low_ref
  30.2 8.1 %collective-permute-done.1.high_ref = f32[6,2,8,1152]{3,2,1,0:T(8,128)S(1)} collective-permute-done((f32[6,2,8,1152]{3,2,1,0:T(8,128)}, f32[6,2,8,1152]{3,2,1,0:T(8,128)S(1)}, u32[]{:S(2)}, u32[]{:S(2)}) %collective-permute-start.1) | collective-permute-done | bytes 442400 | tf_op jit(solution)/shard_map/ppermute | solution.py:306
  38.3 1.2 %shard_map.28 = (f32[3,2,8,2304]{3,2,1,0:T(8,128)S(1)}, f32[3,2,8,2304]{3,2,1,0:T(8,128)S(1)}) custom-call(s32[3]{0:T(128)S(1)} %pad_add_fusion.slab_ref, f32[12,2,8,2304]{3,2,1,0:T(8,128)S(1)} %copy-done, f32[6,2,8,1152]{3,2,1,0:T(8,128)S(1)} %collective-permute-done.low_ref, f32[6,2,8,1152]{3,2,1,0:T(8,128)S(1)} %collective-permute-done.1.high_ref), custom_call_target="tpu_custom_call" | custom-call | tf_op jit(solution)/shard_map/pallas_call | solution.py:323
  39.5 7.8 %collective-permute-start.5 = (f32[3,2,8,2304]{3,2,1,0:T(8,128)S(1)}, f32[3,2,8,2304]{3,2,1,0:T(8,128)S(1)}, u32[]{:S(2)}, u32[]{:S(2)}) collective-permute-start(f32[3,2,8,2304]{3,2,1,0:T(8,128)S(1)} %get-tuple-element.12.inner_ref), channel_id=1, source_target_pairs={{0,1},{1,0},{2,3},{3,2},{4,5},{5,4},{6,7},{7,6},{8,9},{9,8},{10,11... | collective-permute-start | bytes 1327112 | tf_op jit(solution)/shard_map/ppermute | solution.py:332
  47.3 7.7 %collective-permute-start.2 = (f32[3,2,8,2304]{3,2,1,0:T(8,128)S(1)}, f32[3,2,8,2304]{3,2,1,0:T(8,128)S(1)}, u32[]{:S(2)}, u32[]{:S(2)}) collective-permute-start(f32[3,2,8,2304]{3,2,1,0:T(8,128)S(1)} %get-tuple-element.11.outer_ref), channel_id=1, source_target_pairs={{1,2},{2,1},{5,6},{6,5},{9,10},{10,9},{13,14},{14,13},{17,18},{18,... | collective-permute-start | bytes 1327112 | tf_op jit(solution)/shard_map/ppermute | solution.py:331
  55.0 1.0 %shard_map.29 = f32[2,8,128]{2,1,0:T(8,128)S(1)} custom-call(s32[3]{0:T(128)S(1)} %pad_add_fusion.slab_ref, f32[12,2,8,2304]{3,2,1,0:T(8,128)S(1)} %copy-done), custom_call_target="tpu_custom_call" | custom-call | tf_op jit(solution)/shard_map/pallas_call | solution.py:313
  56.0 1.9 %collective-permute-start.6 = (f32[2,8,128]{2,1,0:T(8,128)S(1)}, f32[2,8,128]{2,1,0:T(8,128)S(1)}, u32[]{:S(2)}, u32[]{:S(2)}) collective-permute-start(f32[2,8,128]{2,1,0:T(8,128)S(1)} %shard_map.29), channel_id=1, source_target_pairs={{0,1},{1,0},{2,3},{3,2},{4,5},{5,4},{6,7},{7,6},{8,9},{9,8},{10,11... | collective-permute-start | bytes 24584 | tf_op jit(solution)/shard_map/ppermute | solution.py:320
  57.9 1.1 %collective-permute-done.6 = f32[2,8,128]{2,1,0:T(8,128)S(1)} collective-permute-done((f32[2,8,128]{2,1,0:T(8,128)S(1)}, f32[2,8,128]{2,1,0:T(8,128)S(1)}, u32[]{:S(2)}, u32[]{:S(2)}) %collective-permute-start.6) | collective-permute-done | bytes 8224 | tf_op jit(solution)/shard_map/ppermute | solution.py:320
  59.1 1.9 %collective-permute-start.7 = (f32[2,8,128]{2,1,0:T(8,128)S(1)}, f32[2,8,128]{2,1,0:T(8,128)S(1)}, u32[]{:S(2)}, u32[]{:S(2)}) collective-permute-start(f32[2,8,128]{2,1,0:T(8,128)S(1)} %add.6), channel_id=1, source_target_pairs={{0,3},{1,2},{2,1},{3,0},{4,7},{5,6},{6,5},{7,4},{8,11},{9,10},{10,... | collective-permute-start | bytes 24584 | tf_op jit(solution)/shard_map/ppermute | solution.py:321
  61.0 7.7 %collective-permute-done.7 = f32[2,8,128]{2,1,0:T(8,128)S(1)} collective-permute-done((f32[2,8,128]{2,1,0:T(8,128)S(1)}, f32[2,8,128]{2,1,0:T(8,128)S(1)}, u32[]{:S(2)}, u32[]{:S(2)}) %collective-permute-start.7) | collective-permute-done | bytes 8224 | tf_op jit(solution)/shard_map/ppermute | solution.py:321
  68.7 0.0 copy-done.1
  68.7 0.1 broadcast_in_dim.2.rate_ref
  68.8 0.2 shard_map.30
  69.0 0.0 collective-permute-done.3.low_ref
  69.1 0.0 collective-permute-done.4.high_ref
  69.1 0.0 collective-permute-done.5.halo_ref
  69.1 10.6 %shard_map.31 = (f32[12,2,8,2304]{3,2,1,0:T(8,128)}, f32[7,2,8,2304]{3,2,1,0:T(8,128)S(1)}) custom-call(s32[3]{0:T(128)S(1)} %pad_add_fusion.slab_ref, f32[12,2,8,2304]{3,2,1,0:T(8,128)S(1)} %copy-done, f32[6,2,8,1152]{3,2,1,0:T(8,128)S(1)} %collective-permute-done.3.low_ref, f32[6,2,8,1152]{3,2,1,0:T(8,128)S(1)} %collective-permute-done.4.high_ref, ...), custom_call_target="tpu_custom_call" | custom-call | tf_op jit(solution)/shard_map/pallas_call | solution.py:343
  79.7 0.0 collective-permute-done.2.halo_ref
  79.7 3.6 %shard_map.32 = f32[12,2,8,2304]{3,2,1,0:T(8,128)} custom-call(s32[3]{0:T(128)S(1)} %pad_add_fusion.slab_ref, f32[3,2,8,2304]{3,2,1,0:T(8,128)S(1)} %collective-permute-done.2.halo_ref, f32[3,2,8,2304]{3,2,1,0:T(8,128)S(1)} %get-tuple-element.11.outer_ref, f32[7,2,8,2304]{3,2,1,0:T(8,128)S(1)} %get-tuple-element.15.kept_ref, ...), custom_call_target="tpu_custom_call", output_to_operand_aliasing={{}: (6, {})} | custom-call | tf_op jit(solution)/shard_map/pallas_call | solution.py:361
  (2 shorter events, 0.0 us)
Async XLA Ops:
  0.0 17.8 %copy-start = (f32[12,2,8,2304]{3,2,1,0:T(8,128)S(1)}, f32[12,2,8,2304]{3,2,1,0:T(8,128)}, u32[]{:S(2)}) copy-start(f32[12,2,8,2304]{3,2,1,0:T(8,128)} %f_ref.5) | copy-start | bytes 5308420
  2.3 27.9 %collective-permute-start = (f32[6,2,8,1152]{3,2,1,0:T(8,128)}, f32[6,2,8,1152]{3,2,1,0:T(8,128)S(1)}, u32[]{:S(2)}, u32[]{:S(2)}) collective-permute-start(f32[6,2,8,1152]{3,2,1,0:T(8,128)} %get-tuple-element.22), channel_id=1, source_target_pairs={{0,4},{4,8},{8,12},{12,16},{16,20},{20,24},{24,28},{28,32},{32,36}... | collective-permute-start | bytes 1327112 | tf_op jit(solution)/shard_map/ppermute | solution.py:305
  7.1 31.1 %collective-permute-start.1 = (f32[6,2,8,1152]{3,2,1,0:T(8,128)}, f32[6,2,8,1152]{3,2,1,0:T(8,128)S(1)}, u32[]{:S(2)}, u32[]{:S(2)}) collective-permute-start(f32[6,2,8,1152]{3,2,1,0:T(8,128)} %get-tuple-element.21), channel_id=1, source_target_pairs={{4,0},{8,4},{12,8},{16,12},{20,16},{24,20},{28,24},{32,28},{36,32}... | collective-permute-start | bytes 1327112 | tf_op jit(solution)/shard_map/ppermute | solution.py:306
  18.8 50.3 %collective-permute-start.3 = (f32[6,2,8,1152]{3,2,1,0:T(8,128)}, f32[6,2,8,1152]{3,2,1,0:T(8,128)S(1)}, u32[]{:S(2)}, u32[]{:S(2)}) collective-permute-start(f32[6,2,8,1152]{3,2,1,0:T(8,128)} %get-tuple-element.18), channel_id=1, source_target_pairs={{0,4},{4,8},{8,12},{12,16},{16,20},{20,24},{24,28},{28,32},{32,36}... | collective-permute-start | bytes 1327112 | tf_op jit(solution)/shard_map/ppermute | solution.py:305
  20.7 48.4 %collective-permute-start.4 = (f32[6,2,8,1152]{3,2,1,0:T(8,128)}, f32[6,2,8,1152]{3,2,1,0:T(8,128)S(1)}, u32[]{:S(2)}, u32[]{:S(2)}) collective-permute-start(f32[6,2,8,1152]{3,2,1,0:T(8,128)} %get-tuple-element.17), channel_id=1, source_target_pairs={{4,0},{8,4},{12,8},{16,12},{20,16},{24,20},{28,24},{32,28},{36,32}... | collective-permute-start | bytes 1327112 | tf_op jit(solution)/shard_map/ppermute | solution.py:306
  30.2 38.6 %copy-start.1 = (f32[2,8]{1,0:T(2,128)S(1)}, f32[2,8]{1,0:T(2,128)}, u32[]{:S(2)}) copy-start(f32[2,8]{1,0:T(2,128)} %param.3) | copy-start | bytes 196
  39.5 29.6 %collective-permute-start.5 = (f32[3,2,8,2304]{3,2,1,0:T(8,128)S(1)}, f32[3,2,8,2304]{3,2,1,0:T(8,128)S(1)}, u32[]{:S(2)}, u32[]{:S(2)}) collective-permute-start(f32[3,2,8,2304]{3,2,1,0:T(8,128)S(1)} %get-tuple-element.12.inner_ref), channel_id=1, source_target_pairs={{0,1},{1,0},{2,3},{3,2},{4,5},{5,4},{6,7},{7,6},{8,9},{9,8},{10,11... | collective-permute-start | bytes 1327112 | tf_op jit(solution)/shard_map/ppermute | solution.py:332
  47.3 32.4 %collective-permute-start.2 = (f32[3,2,8,2304]{3,2,1,0:T(8,128)S(1)}, f32[3,2,8,2304]{3,2,1,0:T(8,128)S(1)}, u32[]{:S(2)}, u32[]{:S(2)}) collective-permute-start(f32[3,2,8,2304]{3,2,1,0:T(8,128)S(1)} %get-tuple-element.11.outer_ref), channel_id=1, source_target_pairs={{1,2},{2,1},{5,6},{6,5},{9,10},{10,9},{13,14},{14,13},{17,18},{18,... | collective-permute-start | bytes 1327112 | tf_op jit(solution)/shard_map/ppermute | solution.py:331
  56.0 3.1 %collective-permute-start.6 = (f32[2,8,128]{2,1,0:T(8,128)S(1)}, f32[2,8,128]{2,1,0:T(8,128)S(1)}, u32[]{:S(2)}, u32[]{:S(2)}) collective-permute-start(f32[2,8,128]{2,1,0:T(8,128)S(1)} %shard_map.29), channel_id=1, source_target_pairs={{0,1},{1,0},{2,3},{3,2},{4,5},{5,4},{6,7},{7,6},{8,9},{9,8},{10,11... | collective-permute-start | bytes 24584 | tf_op jit(solution)/shard_map/ppermute | solution.py:320
  59.1 9.7 %collective-permute-start.7 = (f32[2,8,128]{2,1,0:T(8,128)S(1)}, f32[2,8,128]{2,1,0:T(8,128)S(1)}, u32[]{:S(2)}, u32[]{:S(2)}) collective-permute-start(f32[2,8,128]{2,1,0:T(8,128)S(1)} %add.6), channel_id=1, source_target_pairs={{0,3},{1,2},{2,1},{3,0},{4,7},{5,6},{6,5},{7,4},{8,11},{9,10},{10,... | collective-permute-start | bytes 24584 | tf_op jit(solution)/shard_map/ppermute | solution.py:321

commit v2 on v1

v2 whole, which is shorter than its diff:
```python
import functools
import math

import jax
import jax.numpy as jnp
from jax import lax
from jax.experimental import pallas as pl
from jax.experimental.pallas import tpu as pltpu
from jax.sharding import PartitionSpec as P

V = 48
WIDTH = V * V
HALF = WIDTH // 2
DEPTH = 3

vel_max = 4.5
step_ratio = 0.1
collision_scale = 0.004
relax_scale = 0.5
spacing = 2.0 * vel_max / V

VMEM_LIMIT = 40 * 1024 * 1024


def speed_of(position):
    return vel_max * (2.0 * position - (V - 1.0)) / V


def lane_grid(first, width, rows=8):
    lane = lax.broadcasted_iota(jnp.int32, (rows, width), 1).astype(jnp.float32) + float(first)
    column = jnp.floor((lane + 0.5) * (1.0 / V))
    return column, lane - V * column


def wide(tile):
    return jnp.concatenate([tile] * (WIDTH // 128), axis=1)


def moments_kernel(slab_ref, f_ref, out_ref, up_ref, down_ref):
    planes, columns = f_ref.shape[0], f_ref.shape[1]
    slab = slab_ref[0]
    chunk = 768
    lane = lax.broadcasted_iota(jnp.int32, (8, 128), 1)
    for column in range(columns):
        totals = [jnp.zeros((8, 1), jnp.float32)] * 5
        for first in range(0, WIDTH, chunk):
            mass = jnp.zeros((8, chunk), jnp.float32)
            flow = jnp.zeros((8, chunk), jnp.float32)
            heat = jnp.zeros((8, chunk), jnp.float32)
            for plane in range(planes):
                cz = speed_of((slab * planes + plane).astype(jnp.float32))
                f = f_ref[plane, column, :, first : first + chunk]
                scaled = f * cz
                mass += f
                flow += scaled
                heat += scaled * cz
            vx, vy = lane_grid(first, chunk)
            cx, cy = speed_of(vx), speed_of(vy)
            parts = (mass, mass * cx, mass * cy, flow, mass * (cx * cx + cy * cy) + heat)
            totals = [t + jnp.sum(p, axis=1, keepdims=True) for t, p in zip(totals, parts)]
        row = jnp.zeros((8, 128), jnp.float32)
        for k in range(5):
            row = jnp.where(lane == k, totals[k], row)
        out_ref[column] = row
    for k in range(planes - 2 * DEPTH):
        up_ref[k] = f_ref[DEPTH + k, :, :, HALF:]
        down_ref[k] = f_ref[DEPTH + k, :, :, :HALF]


def coefficients_kernel(total_ref, rate_ref, coef_ref, cell_ref):
    for column in range(total_ref.shape[0]):
        m0, m1, m2, m3, m4 = (
            jnp.broadcast_to(total_ref[column, :, k : k + 1], (8, 128)) for k in range(5)
        )
        rate = rate_ref[column]
        density = m0 * spacing**3
        ux, uy, uz = m1 / m0, m2 / m0, m3 / m0
        temperature = (m4 / m0 - ux * ux - uy * uy - uz * uz) / 3.0
        stiff = temperature / (spacing * spacing)
        collide, relax = collision_scale * rate, relax_scale * rate
        inverse = 1.0 / (1.0 + relax + 6.0 * collide * stiff)
        middle = collide * inverse * (stiff + 0.5)
        slope = collide * inverse * (0.5 / spacing)
        root = 1.0 / jnp.sqrt(2.0 * math.pi * temperature)
        scale = density * (root * root * root) * (relax * inverse)
        for k, value in enumerate((middle, slope, uz, temperature, inverse)):
            cell_ref[column, k] = value
        vx, vy = lane_grid(0, WIDTH)
        dx, dy = speed_of(vx) - wide(ux), speed_of(vy) - wide(uy)
        middle, slope = wide(middle), wide(slope)
        coef_ref[column, 0] = jnp.where(vx < V - 1.5, middle + slope * dx, 0.0)
        coef_ref[column, 1] = jnp.where(vx > 0.5, middle - slope * dx, 0.0)
        coef_ref[column, 2] = jnp.where(vy < V - 1.5, middle + slope * dy, 0.0)
        coef_ref[column, 3] = jnp.where(vy > 0.5, middle - slope * dy, 0.0)
        coef_ref[column, 4] = wide(scale) * jnp.exp(
            -(dx * dx + dy * dy) / (2.0 * wide(temperature))
        )


def upwind_weights(speed):
    a = step_ratio * jnp.abs(speed)
    return 1.0 - 1.5 * a + 0.5 * a * a, 2.0 * a - a * a, 0.5 * a * a - 0.5 * a


def fill_weights(weight_ref):
    vx, vy = lane_grid(0, WIDTH)
    for k, value in enumerate(upwind_weights(speed_of(vx)) + upwind_weights(speed_of(vy))):
        weight_ref[k] = value
    weight_ref[6] = jnp.where(vy > V // 2 - 0.5, 1.0, 0.0)


def transport_plane(f_ref, plane, low_ref, high_ref, entry, weight_ref, store):
    for column in range(2):
        for part in range(2):
            lanes = pl.ds(part * HALF, HALF)
            f = f_ref[plane, column, :, lanes]
            if part == 1:
                near = low_ref[entry, 1] if column == 0 else f_ref[plane, 0, :, lanes]
                far = low_ref[entry, column]
            else:
                near = f_ref[plane, 1, :, lanes] if column == 0 else high_ref[entry, 0]
                far = high_ref[entry, column]
            swept = (
                weight_ref[0, :, lanes] * f
                + weight_ref[1, :, lanes] * near
                + weight_ref[2, :, lanes] * far
            )
            positive = weight_ref[6, :, lanes] > 0.5
            near = jnp.where(positive, pltpu.roll(swept, 1, 0), pltpu.roll(swept, 7, 0))
            far = jnp.where(positive, pltpu.roll(swept, 2, 0), pltpu.roll(swept, 6, 0))
            store(
                column,
                lanes,
                weight_ref[3, :, lanes] * swept
                + weight_ref[4, :, lanes] * near
                + weight_ref[5, :, lanes] * far,
            )


def edges_kernel(slab_ref, f_ref, low_ref, high_ref, outer_ref, inner_ref, weight_ref):
    planes = f_ref.shape[0]
    odd = lax.rem(slab_ref[0], 2)
    fill_weights(weight_ref)
    for side, target in ((0, outer_ref), (1, inner_ref)):

        def step(k, carry, side=side, target=target):
            place = k + side * DEPTH
            entry = jnp.where(odd == 1, 2 * DEPTH - 1 - place, place)
            plane = jnp.where(entry < DEPTH, entry, entry + planes - 2 * DEPTH)

            def store(column, lanes, value):
                target[k, column, :, lanes] = value

            transport_plane(f_ref, plane, low_ref, high_ref, entry, weight_ref, store)
            return carry

        lax.fori_loop(0, DEPTH, step, 0)


CHUNK = 9


def neighbours(tiles):
    lane = lax.broadcasted_iota(jnp.int32, (8, 128), 1)
    found = []
    for distance in (V, 1):
        ahead = [pltpu.roll(t, 128 - distance, 1) for t in tiles[1:]]
        behind = [pltpu.roll(t, distance, 1) for t in tiles[:-1]]
        inner, outer = lane < 128 - distance, lane >= distance
        found.append([jnp.where(inner, ahead[k], ahead[k + 1]) for k in range(CHUNK)])
        found.append([jnp.where(outer, behind[k + 1], behind[k]) for k in range(CHUNK)])
    return found


class Cell:
    def __init__(self, cell_ref, column, slab, planes):
        odd = lax.rem(slab, 2)
        self.middle, self.slope, self.uz, self.temperature, self.inverse = (
            cell_ref[column, k] for k in range(5)
        )
        self.sign = jnp.where(odd == 1, -1.0, 1.0)
        self.zero = speed_of((slab * planes + odd * (planes - 1)).astype(jnp.float32))

    def distance(self, place):
        return self.zero + self.sign * (place * spacing) - self.uz

    def weights(self, place):
        tilt = self.sign * self.slope * self.distance(place)
        return self.middle + tilt, self.middle - tilt

    def fall(self, place):
        distance = self.distance(place)
        return jnp.exp(-(distance * distance) / (2.0 * self.temperature))


def sweep(places, old, new, source, coef_ref, cell_ref, slab, planes, make=False, also=None):
    per_row = WIDTH // (128 * CHUNK)

    def at(pair, column, first):
        if pair is None:
            return None
        ref, index = pair
        return ref[index, column, :, pl.ds(first, 128)]

    def step(item, carry):
        column = item // per_row
        base = (item - column * per_row) * (128 * CHUNK)
        firsts = [pl.multiple_of(base + 128 * k, 128) for k in range(CHUNK)]
        left = pl.multiple_of(jnp.maximum(base - 128, 0), 128)
        right = pl.multiple_of(jnp.minimum(base + 128 * CHUNK, WIDTH - 128), 128)
        count = 5 if make else 4
        coef = [[coef_ref[column, k, :, pl.ds(f, 128)] for f in firsts] for k in range(count)]
        cell = Cell(cell_ref, column, slab, planes)
        before = [at(old(places[0] - 1), column, f) for f in firsts]
        here = [at(old(places[0]), column, f) for f in firsts]
        for place in places:
            after = [at(old(place + 1), column, f) for f in firsts]
            ends = [at(old(place), column, f) for f in (left, right)]
            shifted = neighbours([ends[0], *here, ends[1]])
            plus, minus = cell.weights(place)
            if make:
                fall = cell.fall(place)
            targets = [new(place)]
            if also is not None and also(place) is not None:
                targets.append(also(place))
            for k, f in enumerate(firsts):
                if make:
                    total = cell.inverse * here[k] + fall * coef[4][k]
                    ref, index = source(place)
                    ref[index, column, :, pl.ds(f, 128)] = total
                else:
                    total = at(source(place), column, f)
                side = plus * after[k]
                if before[k] is not None:
                    side += minus * before[k]
                across = coef[0][k] * shifted[0][k] + coef[1][k] * shifted[1][k]
                along = coef[2][k] * shifted[2][k] + coef[3][k] * shifted[3][k]
                total = (total + side) + (across + along)
                for ref, index in targets:
                    ref[index, column, :, pl.ds(f, 128)] = total
            before, here = here, after
        return carry

    lax.fori_loop(0, 2 * per_row, step, 0)


def main_kernel(
    slab_ref, f_ref, low_ref, high_ref, outer_ref, inner_ref, halo_ref, coef_ref, cell_ref,
    out_ref, kept_ref, weight_ref, zero_ref, source_ref, one_ref, two_ref, new_ref, sem,
):
    planes = f_ref.shape[0]
    slab = slab_ref[0]
    odd = lax.rem(slab, 2)
    fill_weights(weight_ref)

    def transport_step(k, carry):
        plane = jnp.where(odd == 1, planes - 1 - DEPTH - k, DEPTH + k)

        def store(column, lanes, value):
            zero_ref[k, column, :, lanes] = value

        transport_plane(f_ref, plane, low_ref, high_ref, plane - DEPTH, weight_ref, store)
        return carry

    lax.fori_loop(0, planes - 2 * DEPTH, transport_step, 0)

    def start_of(place):
        if place < 0:
            return None
        if place < DEPTH:
            return outer_ref, place
        if place < planes - DEPTH:
            return zero_ref, place - DEPTH
        if place < planes:
            return inner_ref, place - planes + DEPTH
        return halo_ref, planes + DEPTH - 1 - place

    def one(place):
        return None if place < 0 else (one_ref, place)

    def two(place):
        return None if place < 0 else (two_ref, place)

    def source(place):
        return source_ref, place

    def last(place):
        if place < DEPTH:
            return kept_ref, place + 1
        return new_ref, jnp.where(odd == 1, planes - 1 - place, place - DEPTH)

    def first(place):
        return (kept_ref, 0) if place == 0 else None

    rest = (coef_ref, cell_ref, slab, planes)
    sweep(range(0, planes + 2), start_of, one, source, *rest, make=True, also=first)
    sweep(range(0, planes + 1), one, two, source, *rest)
    sweep(range(0, planes), two, last, source, *rest)
    done = pltpu.make_async_copy(
        new_ref, out_ref.at[pl.ds((1 - odd) * DEPTH, planes - DEPTH)], sem
    )
    done.start()
    done.wait()


def last_kernel(
    slab_ref, halo_ref, outer_ref, kept_ref, coef_ref, cell_ref, before_ref,
    out_ref, new_ref, mix_ref, rest_ref, sem,
):
    planes = out_ref.shape[0]
    slab = slab_ref[0]
    odd = lax.rem(slab, 2)
    inside = jnp.where((slab == 0) | (slab == slab_ref[1] - 1), 0.0, 1.0)
    per_row = WIDTH // (128 * CHUNK)

    def spot(place):
        return jnp.where(odd == 1, DEPTH - 1 - place, place)

    def within(read, coef_ref, column, base, firsts):
        left = pl.multiple_of(jnp.maximum(base - 128, 0), 128)
        right = pl.multiple_of(jnp.minimum(base + 128 * CHUNK, WIDTH - 128), 128)
        tiles = [read(f) for f in (left, *firsts, right)]
        shifted = neighbours(tiles)
        results = []
        for k, f in enumerate(firsts):
            coef = [coef_ref[column, c, :, pl.ds(f, 128)] for c in range(4)]
            results.append(
                (coef[0] * shifted[0][k] + coef[1] * shifted[1][k])
                + (coef[2] * shifted[2][k] + coef[3] * shifted[3][k])
            )
        return results

    def walk(body):
        def step(item, carry):
            column = item // per_row
            base = (item - column * per_row) * (128 * CHUNK)
            firsts = [pl.multiple_of(base + 128 * k, 128) for k in range(CHUNK)]
            cell = Cell(cell_ref, column, slab, planes)
            body(column, base, firsts, cell)
            return carry

        lax.fori_loop(0, 2 * per_row, step, 0)

    def first(column, base, firsts, cell):
        plus1, minus1 = cell.weights(-1)
        plus2, minus2 = cell.weights(-2)
        next0, into0 = cell.weights(0)
        _, into1 = cell.weights(1)
        _, into2 = cell.weights(2)
        into0 = into0 * inside
        fall1, fall2 = cell.fall(-1), cell.fall(-2)
        flat = within(lambda f: halo_ref[0, column, :, pl.ds(f, 128)], coef_ref, column, base, firsts)
        for k, f in enumerate(firsts):
            lanes = pl.ds(f, 128)
            h1, h2, h3 = (halo_ref[i, column, :, lanes] for i in range(3))
            bell = coef_ref[column, 4, :, lanes]
            source1 = cell.inverse * h1 + fall1 * bell
            source2 = cell.inverse * h2 + fall2 * bell
            swept = minus1 * h2 + flat[k]
            once = source1 + plus1 * outer_ref[0, column, :, lanes] + swept
            mix_ref[column, :, lanes] = swept + 2.0 * once
            own = kept_ref[0, column, :, lanes] + into0 * h1
            other = source2 + plus2 * h1 + minus2 * h3
            rest_ref[column, :, lanes] = (
                kept_ref[1, column, :, lanes]
                + (next0 * into1 * into0) * h1
                + into0 * (source1 + plus1 * own + minus1 * other)
            )
            new_ref[spot(1), column, :, lanes] = kept_ref[2, column, :, lanes] + (into1 * into0) * (
                once + 2.0 * flat[k]
            )
            new_ref[spot(2), column, :, lanes] = (
                kept_ref[3, column, :, lanes] + (into2 * into1 * into0) * h1
            )

    def second(column, base, firsts, cell):
        into0 = cell.weights(0)[1] * inside
        flat = within(lambda f: mix_ref[column, :, pl.ds(f, 128)], coef_ref, column, base, firsts)
        for k, f in enumerate(firsts):
            lanes = pl.ds(f, 128)
            new_ref[spot(0), column, :, lanes] = rest_ref[column, :, lanes] + into0 * flat[k]

    walk(first)
    walk(second)
    done = pltpu.make_async_copy(
        new_ref, out_ref.at[pl.ds(odd * (planes - DEPTH), DEPTH)], sem
    )
    done.start()
    done.wait()


def shape(*dims):
    return jax.ShapeDtypeStruct(dims, jnp.float32)


PARAMS = pltpu.CompilerParams(vmem_limit_bytes=VMEM_LIMIT)
HEAVY = pl.CostEstimate(flops=20_000_000_000, bytes_accessed=20_000_000, transcendentals=0)
SMEM = pl.BlockSpec(memory_space=pltpu.SMEM)
VMEM = pl.BlockSpec(memory_space=pltpu.VMEM)
ANY = pl.BlockSpec(memory_space=pl.ANY)


def shards(distribution, collision_rate):
    planes, columns, rows, width = distribution.shape
    spaces, slabs = lax.axis_size("space"), lax.axis_size("vz")
    slab = lax.axis_index("vz").astype(jnp.int32)
    facts = jnp.stack([slab, jnp.int32(slabs)])

    forward = [(i, (i + 1) % spaces) for i in range(spaces)]
    backward = [(b, a) for a, b in forward]
    partners = [(i, i ^ 1) for i in range(slabs)]
    crossing = [(i, i + 1) for i in range(1, slabs - 1, 2)]
    crossing += [(b, a) for a, b in crossing]
    opposite = [(i, slabs - 1 - i) for i in range(slabs)]

    def both_ways(up, down):
        return lax.ppermute(up, "space", forward), lax.ppermute(down, "space", backward)

    groups = distribution.reshape(planes // DEPTH, DEPTH, columns, rows, width)
    groups = groups[:: planes // DEPTH - 1]
    ends = (2 * DEPTH, columns, rows, HALF)
    up, down, later = lax.optimization_barrier(
        (groups[..., HALF:].reshape(ends), groups[..., :HALF].reshape(ends), distribution)
    )
    edge_low, edge_high = both_ways(up, down)

    half = (planes - 2 * DEPTH, columns, rows, HALF)
    part, up, down = pl.pallas_call(
        moments_kernel,
        out_shape=[shape(columns, rows, 128), shape(*half), shape(*half)],
        in_specs=[SMEM, VMEM],
        out_specs=[VMEM] * 3,
        compiler_params=PARAMS,
    )(facts, later)
    low, high = both_ways(up, down)
    part = part + lax.ppermute(part, "vz", partners)
    edge_low, edge_high, _ = lax.optimization_barrier((edge_low, edge_high, part))
    total = part + lax.ppermute(part, "vz", opposite)

    outer, inner = pl.pallas_call(
        edges_kernel,
        out_shape=[shape(DEPTH, columns, rows, width)] * 2,
        in_specs=[SMEM, VMEM, VMEM, VMEM],
        out_specs=[VMEM, VMEM],
        scratch_shapes=[pltpu.VMEM((7, rows, width), jnp.float32)],
        compiler_params=PARAMS,
        cost_estimate=HEAVY,
    )(facts, distribution, edge_low, edge_high)
    outer_halo = lax.ppermute(outer, "vz", crossing)
    inner_halo = lax.ppermute(inner, "vz", partners)

    coef, cell = pl.pallas_call(
        coefficients_kernel,
        out_shape=[shape(columns, 5, rows, width), shape(columns, 5, rows, 128)],
        in_specs=[VMEM, VMEM],
        out_specs=[VMEM, VMEM],
        compiler_params=PARAMS,
        cost_estimate=HEAVY,
    )(total, jnp.broadcast_to(collision_rate[:, :, None], (columns, rows, 128)))

    block = (columns, rows, width)
    most, kept = pl.pallas_call(
        main_kernel,
        out_shape=[shape(planes, *block), shape(4, *block)],
        in_specs=[SMEM] + [VMEM] * 8,
        out_specs=[ANY, VMEM],
        scratch_shapes=[
            pltpu.VMEM((7, rows, width), jnp.float32),
            pltpu.VMEM((planes - 2 * DEPTH, *block), jnp.float32),
            pltpu.VMEM((planes + 2, *block), jnp.float32),
            pltpu.VMEM((planes + 2, *block), jnp.float32),
            pltpu.VMEM((planes + 1, *block), jnp.float32),
            pltpu.VMEM((planes - DEPTH, *block), jnp.float32),
            pltpu.SemaphoreType.DMA,
        ],
        compiler_params=PARAMS,
        cost_estimate=HEAVY,
    )(facts, distribution, low, high, outer, inner, inner_halo, coef, cell)

    return pl.pallas_call(
        last_kernel,
        out_shape=shape(planes, *block),
        in_specs=[SMEM] + [VMEM] * 5 + [ANY],
        out_specs=ANY,
        scratch_shapes=[
            pltpu.VMEM((DEPTH, *block), jnp.float32),
            pltpu.VMEM(block, jnp.float32),
            pltpu.VMEM(block, jnp.float32),
            pltpu.SemaphoreType.DMA,
        ],
        input_output_aliases={6: 0},
        compiler_params=PARAMS,
    )(facts, outer_halo, outer, kept, coef, cell, most)


def solution(mesh):
    return jax.shard_map(
        shards,
        mesh=mesh,
        in_specs=(P("vz", "space", None, None), P("space", None)),
        out_specs=P("vz", "space", None, None),
        check_vma=False,
    )
```

time: 83.6 us -> 69.3 us (0.83)
  the two profiles are of different devices: /device:TPU:1 before, /device:TPU:69 now
where the time goes in v2:
time: 69.3 us; the launch traced here: 69 us
  starting transfers between devices  32.1 us (46%)
  waiting for transfers between devices  20.3 us (29%)
  Pallas kernels  14.9 us (22%)
  local copies, waits for them, and re-layouts  1.5 us (2%)
    ppermute x1, waiting for transfers between devices, shards(): total = part + lax.ppermute(part, 'vz', opposite)  15 us
    pallas_call x1, Pallas kernels, shards(): pl.pallas_call(main_kernel, out_shape=[shape(planes, *block), shape(4, *b...  10.1 us
    ppermute x1, starting transfers between devices, shards(): total = part + lax.ppermute(part, 'vz', opposite)  9.6 us
    ppermute x2, starting transfers between devices, both_ways(): lax.ppermute(down, 'space', backward)  7.73 us
    ppermute x2, starting transfers between devices, both_ways(): lax.ppermute(up, 'space', forward)  7.1 us
    ppermute x1, waiting for transfers between devices, shards(): outer_halo = lax.ppermute(outer, 'vz', crossing)  4.48 us
    ppermute x1, starting transfers between devices, shards(): outer_halo = lax.ppermute(outer, 'vz', crossing)  2.93 us
    ppermute x1, starting transfers between devices, shards(): part = part + lax.ppermute(part, 'vz', partners)  2.85 us
  transfers between devices with their start and end apart: 8, of which 3 were waited for; matrix products, arithmetic and copies ran while one was open for 0% of the time, Pallas kernels for 18%

profile of v2, /device:TPU:69, one launch (start us, length us, event | category | flops | bytes accessed | tf_op | source)
XLA Modules:
  0.0 69.0 jit_solution(12936882867874195712)
XLA Ops:
  0.0 0.0 copy-start
  0.0 1.4 %slice.9 = f32[2,3,2,8,2304]{4,3,2,1,0:T(8,128)S(1)} slice(f32[4,3,2,8,2304]{4,3,2,1,0:T(8,128)} %bitcast.4), slice={[0:4:3], [0:3:1], [0:2:1], [0:8:1], [0:2304:1]} | slice | bytes 1769472 | tf_op jit(solution)/shard_map/slice | solution.py:420
  1.4 0.1 fusion
  1.4 4.0 %collective-permute-start = (f32[6,2,8,1152]{3,2,1,0:T(8,128)S(1)}, f32[6,2,8,1152]{3,2,1,0:T(8,128)S(1)}, u32[]{:S(2)}, u32[]{:S(2)}) collective-permute-start(f32[6,2,8,1152]{3,2,1,0:T(8,128)S(1)} %bitcast.6), channel_id=1, source_target_pairs={{0,4},{4,8},{8,12},{12,16},{16,20},{20,24},{24,28},{28,32},{32,36}... | collective-permute-start | bytes 1327112 | tf_op jit(solution)/shard_map/ppermute | solution.py:417
  5.4 1.9 %collective-permute-start.1 = (f32[6,2,8,1152]{3,2,1,0:T(8,128)S(1)}, f32[6,2,8,1152]{3,2,1,0:T(8,128)S(1)}, u32[]{:S(2)}, u32[]{:S(2)}) collective-permute-start(f32[6,2,8,1152]{3,2,1,0:T(8,128)S(1)} %bitcast.5), channel_id=1, source_target_pairs={{4,0},{8,4},{12,8},{16,12},{20,16},{24,20},{28,24},{32,28},{36,32}... | collective-permute-start | bytes 1327112 | tf_op jit(solution)/shard_map/ppermute | solution.py:417
  7.4 0.1 pad_add_fusion.slab_ref
  7.4 0.0 copy-done
  7.5 1.0 %shard_map.28 = (f32[2,8,128]{2,1,0:T(8,128)S(1)}, f32[6,2,8,1152]{3,2,1,0:T(8,128)S(1)}, f32[6,2,8,1152]{3,2,1,0:T(8,128)S(1)}) custom-call(s32[2]{0:T(128)S(1)} %pad_add_fusion.slab_ref, f32[12,2,8,2304]{3,2,1,0:T(8,128)S(1)} %copy-done), custom_call_target="tpu_custom_call" | custom-call | tf_op jit(solution)/shard_map/pallas_call | solution.py:428
  8.5 2.9 %collective-permute-start.2 = (f32[2,8,128]{2,1,0:T(8,128)S(1)}, f32[2,8,128]{2,1,0:T(8,128)S(1)}, u32[]{:S(2)}, u32[]{:S(2)}) collective-permute-start(f32[2,8,128]{2,1,0:T(8,128)S(1)} %get-tuple-element.22), channel_id=1, source_target_pairs={{0,1},{1,0},{2,3},{3,2},{4,5},{5,4},{6,7},{7,6},{8,9},{9,8},{10,11... | collective-permute-start | bytes 24584 | tf_op jit(solution)/shard_map/ppermute | solution.py:436
  11.3 0.8 %collective-permute-done.2 = f32[2,8,128]{2,1,0:T(8,128)S(1)} collective-permute-done((f32[2,8,128]{2,1,0:T(8,128)S(1)}, f32[2,8,128]{2,1,0:T(8,128)S(1)}, u32[]{:S(2)}, u32[]{:S(2)}) %collective-permute-start.2) | collective-permute-done | bytes 8224 | tf_op jit(solution)/shard_map/ppermute | solution.py:436
  12.1 9.6 %collective-permute-start.7 = (f32[2,8,128]{2,1,0:T(8,128)S(1)}, f32[2,8,128]{2,1,0:T(8,128)S(1)}, u32[]{:S(2)}, u32[]{:S(2)}) collective-permute-start(f32[2,8,128]{2,1,0:T(8,128)S(1)} %add.6), channel_id=1, source_target_pairs={{0,3},{1,2},{2,1},{3,0},{4,7},{5,6},{6,5},{7,4},{8,11},{9,10},{10,... | collective-permute-start | bytes 24584 | tf_op jit(solution)/shard_map/ppermute | solution.py:438
  21.7 3.1 %collective-permute-start.4 = (f32[6,2,8,1152]{3,2,1,0:T(8,128)S(1)}, f32[6,2,8,1152]{3,2,1,0:T(8,128)S(1)}, u32[]{:S(2)}, u32[]{:S(2)}) collective-permute-start(f32[6,2,8,1152]{3,2,1,0:T(8,128)S(1)} %get-tuple-element.26), channel_id=1, source_target_pairs={{0,4},{4,8},{8,12},{12,16},{16,20},{20,24},{24,28},{28,32},{32,36}... | collective-permute-start | bytes 1327112 | tf_op jit(solution)/shard_map/ppermute | solution.py:417
  24.8 5.8 %collective-permute-start.5 = (f32[6,2,8,1152]{3,2,1,0:T(8,128)S(1)}, f32[6,2,8,1152]{3,2,1,0:T(8,128)S(1)}, u32[]{:S(2)}, u32[]{:S(2)}) collective-permute-start(f32[6,2,8,1152]{3,2,1,0:T(8,128)S(1)} %get-tuple-element.27), channel_id=1, source_target_pairs={{4,0},{8,4},{12,8},{16,12},{20,16},{24,20},{28,24},{32,28},{36,32}... | collective-permute-start | bytes 1327112 | tf_op jit(solution)/shard_map/ppermute | solution.py:417
  30.7 15.0 %collective-permute-done.7 = f32[2,8,128]{2,1,0:T(8,128)S(1)} collective-permute-done((f32[2,8,128]{2,1,0:T(8,128)S(1)}, f32[2,8,128]{2,1,0:T(8,128)S(1)}, u32[]{:S(2)}, u32[]{:S(2)}) %collective-permute-start.7) | collective-permute-done | bytes 8224 | tf_op jit(solution)/shard_map/ppermute | solution.py:438
  45.7 0.0 copy-start.1
  45.7 0.0 collective-permute-done.low_ref
  45.7 0.0 collective-permute-done.1.high_ref
  45.7 1.2 %shard_map.29 = (f32[3,2,8,2304]{3,2,1,0:T(8,128)S(1)}, f32[3,2,8,2304]{3,2,1,0:T(8,128)S(1)}) custom-call(s32[2]{0:T(128)S(1)} %pad_add_fusion.slab_ref, f32[12,2,8,2304]{3,2,1,0:T(8,128)S(1)} %copy-done, f32[6,2,8,1152]{3,2,1,0:T(8,128)S(1)} %collective-permute-done.low_ref, f32[6,2,8,1152]{3,2,1,0:T(8,128)S(1)} %collective-permute-done.1.high_ref), custom_call_target="tpu_custom_call" | custom-call | flops 20000000000 | bytes 20000000 | tf_op jit(solution)/shard_map/pallas_call | solution.py:440
  46.9 1.9 %collective-permute-start.6 = (f32[3,2,8,2304]{3,2,1,0:T(8,128)S(1)}, f32[3,2,8,2304]{3,2,1,0:T(8,128)S(1)}, u32[]{:S(2)}, u32[]{:S(2)}) collective-permute-start(f32[3,2,8,2304]{3,2,1,0:T(8,128)S(1)} %get-tuple-element.28.inner_ref), channel_id=1, source_target_pairs={{0,1},{1,0},{2,3},{3,2},{4,5},{5,4},{6,7},{7,6},{8,9},{9,8},{10,11... | collective-permute-start | bytes 1327112 | tf_op jit(solution)/shard_map/ppermute | solution.py:450
  48.8 0.0 copy-done.1
  48.8 0.1 broadcast_in_dim.2.rate_ref
  48.9 0.2 shard_map.30
  49.1 2.9 %collective-permute-start.3 = (f32[3,2,8,2304]{3,2,1,0:T(8,128)S(1)}, f32[3,2,8,2304]{3,2,1,0:T(8,128)S(1)}, u32[]{:S(2)}, u32[]{:S(2)}) collective-permute-start(f32[3,2,8,2304]{3,2,1,0:T(8,128)S(1)} %get-tuple-element.25.outer_ref), channel_id=1, source_target_pairs={{1,2},{2,1},{5,6},{6,5},{9,10},{10,9},{13,14},{14,13},{17,18},{18,... | collective-permute-start | bytes 1327112 | tf_op jit(solution)/shard_map/ppermute | solution.py:449
  52.1 0.0 collective-permute-done.4.low_ref
  52.1 0.0 collective-permute-done.5.high_ref
  52.1 0.0 collective-permute-done.6.halo_ref
  52.1 10.1 %shard_map.31 = (f32[12,2,8,2304]{3,2,1,0:T(8,128)}, f32[4,2,8,2304]{3,2,1,0:T(8,128)S(1)}) custom-call(s32[2]{0:T(128)S(1)} %pad_add_fusion.slab_ref, f32[12,2,8,2304]{3,2,1,0:T(8,128)S(1)} %copy-done, f32[6,2,8,1152]{3,2,1,0:T(8,128)S(1)} %collective-permute-done.4.low_ref, f32[6,2,8,1152]{3,2,1,0:T(8,128)S(1)} %collective-permute-done.5.high_ref, ...), custom_call_target="tpu_custom_call" | custom-call | flops 20000000000 | bytes 20000000 | tf_op jit(solution)/shard_map/pallas_call | solution.py:462
  62.2 4.5 %collective-permute-done.3.halo_ref = f32[3,2,8,2304]{3,2,1,0:T(8,128)S(1)} collective-permute-done((f32[3,2,8,2304]{3,2,1,0:T(8,128)S(1)}, f32[3,2,8,2304]{3,2,1,0:T(8,128)S(1)}, u32[]{:S(2)}, u32[]{:S(2)}) %collective-permute-start.3) | collective-permute-done | bytes 442400 | tf_op jit(solution)/shard_map/ppermute | solution.py:449
  66.7 2.3 %shard_map.32 = f32[12,2,8,2304]{3,2,1,0:T(8,128)} custom-call(s32[2]{0:T(128)S(1)} %pad_add_fusion.slab_ref, f32[3,2,8,2304]{3,2,1,0:T(8,128)S(1)} %collective-permute-done.3.halo_ref, f32[3,2,8,2304]{3,2,1,0:T(8,128)S(1)} %get-tuple-element.25.outer_ref, f32[4,2,8,2304]{3,2,1,0:T(8,128)S(1)} %get-tuple-element.31.kept_ref, ...), custom_call_target="tpu_custom_call", output_to_operand_aliasing={{}: (6, {})} | custom-call | tf_op jit(solution)/shard_map/pallas_call | solution.py:480
  (2 shorter events, 0.0 us)
Async XLA Ops:
  0.0 7.4 %copy-start = (f32[12,2,8,2304]{3,2,1,0:T(8,128)S(1)}, f32[12,2,8,2304]{3,2,1,0:T(8,128)}, u32[]{:S(2)}) copy-start(f32[12,2,8,2304]{3,2,1,0:T(8,128)} %f_ref.4) | copy-start | bytes 5308420
  1.4 44.3 %collective-permute-start = (f32[6,2,8,1152]{3,2,1,0:T(8,128)S(1)}, f32[6,2,8,1152]{3,2,1,0:T(8,128)S(1)}, u32[]{:S(2)}, u32[]{:S(2)}) collective-permute-start(f32[6,2,8,1152]{3,2,1,0:T(8,128)S(1)} %bitcast.6), channel_id=1, source_target_pairs={{0,4},{4,8},{8,12},{12,16},{16,20},{20,24},{24,28},{28,32},{32,36}... | collective-permute-start | bytes 1327112 | tf_op jit(solution)/shard_map/ppermute | solution.py:417
  5.4 40.3 %collective-permute-start.1 = (f32[6,2,8,1152]{3,2,1,0:T(8,128)S(1)}, f32[6,2,8,1152]{3,2,1,0:T(8,128)S(1)}, u32[]{:S(2)}, u32[]{:S(2)}) collective-permute-start(f32[6,2,8,1152]{3,2,1,0:T(8,128)S(1)} %bitcast.5), channel_id=1, source_target_pairs={{4,0},{8,4},{12,8},{16,12},{20,16},{24,20},{28,24},{32,28},{36,32}... | collective-permute-start | bytes 1327112 | tf_op jit(solution)/shard_map/ppermute | solution.py:417
  8.5 3.7 %collective-permute-start.2 = (f32[2,8,128]{2,1,0:T(8,128)S(1)}, f32[2,8,128]{2,1,0:T(8,128)S(1)}, u32[]{:S(2)}, u32[]{:S(2)}) collective-permute-start(f32[2,8,128]{2,1,0:T(8,128)S(1)} %get-tuple-element.22), channel_id=1, source_target_pairs={{0,1},{1,0},{2,3},{3,2},{4,5},{5,4},{6,7},{7,6},{8,9},{9,8},{10,11... | collective-permute-start | bytes 24584 | tf_op jit(solution)/shard_map/ppermute | solution.py:436
  12.1 33.5 %collective-permute-start.7 = (f32[2,8,128]{2,1,0:T(8,128)S(1)}, f32[2,8,128]{2,1,0:T(8,128)S(1)}, u32[]{:S(2)}, u32[]{:S(2)}) collective-permute-start(f32[2,8,128]{2,1,0:T(8,128)S(1)} %add.6), channel_id=1, source_target_pairs={{0,3},{1,2},{2,1},{3,0},{4,7},{5,6},{6,5},{7,4},{8,11},{9,10},{10,... | collective-permute-start | bytes 24584 | tf_op jit(solution)/shard_map/ppermute | solution.py:438
  21.7 30.3 %collective-permute-start.4 = (f32[6,2,8,1152]{3,2,1,0:T(8,128)S(1)}, f32[6,2,8,1152]{3,2,1,0:T(8,128)S(1)}, u32[]{:S(2)}, u32[]{:S(2)}) collective-permute-start(f32[6,2,8,1152]{3,2,1,0:T(8,128)S(1)} %get-tuple-element.26), channel_id=1, source_target_pairs={{0,4},{4,8},{8,12},{12,16},{16,20},{20,24},{24,28},{28,32},{32,36}... | collective-permute-start | bytes 1327112 | tf_op jit(solution)/shard_map/ppermute | solution.py:417
  24.8 27.2 %collective-permute-start.5 = (f32[6,2,8,1152]{3,2,1,0:T(8,128)S(1)}, f32[6,2,8,1152]{3,2,1,0:T(8,128)S(1)}, u32[]{:S(2)}, u32[]{:S(2)}) collective-permute-start(f32[6,2,8,1152]{3,2,1,0:T(8,128)S(1)} %get-tuple-element.27), channel_id=1, source_target_pairs={{4,0},{8,4},{12,8},{16,12},{20,16},{24,20},{28,24},{32,28},{36,32}... | collective-permute-start | bytes 1327112 | tf_op jit(solution)/shard_map/ppermute | solution.py:417
  45.7 3.1 %copy-start.1 = (f32[2,8]{1,0:T(2,128)S(1)}, f32[2,8]{1,0:T(2,128)}, u32[]{:S(2)}) copy-start(f32[2,8]{1,0:T(2,128)} %param.3) | copy-start | bytes 196
  46.9 5.2 %collective-permute-start.6 = (f32[3,2,8,2304]{3,2,1,0:T(8,128)S(1)}, f32[3,2,8,2304]{3,2,1,0:T(8,128)S(1)}, u32[]{:S(2)}, u32[]{:S(2)}) collective-permute-start(f32[3,2,8,2304]{3,2,1,0:T(8,128)S(1)} %get-tuple-element.28.inner_ref), channel_id=1, source_target_pairs={{0,1},{1,0},{2,3},{3,2},{4,5},{5,4},{6,7},{7,6},{8,9},{9,8},{10,11... | collective-permute-start | bytes 1327112 | tf_op jit(solution)/shard_map/ppermute | solution.py:450
  49.1 17.6 %collective-permute-start.3 = (f32[3,2,8,2304]{3,2,1,0:T(8,128)S(1)}, f32[3,2,8,2304]{3,2,1,0:T(8,128)S(1)}, u32[]{:S(2)}, u32[]{:S(2)}) collective-permute-start(f32[3,2,8,2304]{3,2,1,0:T(8,128)S(1)} %get-tuple-element.25.outer_ref), channel_id=1, source_target_pairs={{1,2},{2,1},{5,6},{6,5},{9,10},{10,9},{13,14},{14,13},{17,18},{18,... | collective-permute-start | bytes 1327112 | tf_op jit(solution)/shard_map/ppermute | solution.py:449

commit v3 on v2

--- a/solution.py
+++ b/solution.py
@@ -380,13 +380,22 @@
             lanes = pl.ds(f, 128)
             new_ref[spot(0), column, :, lanes] = rest_ref[column, :, lanes] + into0 * flat[k]
 
+    def copy(place, count, sem):
+        held = jnp.where(odd == 1, DEPTH - place - count, place)
+        return pltpu.make_async_copy(
+            new_ref.at[pl.ds(held, count)],
+            out_ref.at[pl.ds(held + odd * (planes - DEPTH), count)],
+            sem,
+        )
+
     walk(first)
+    outer = copy(1, DEPTH - 1, sem.at[1])
+    outer.start()
     walk(second)
-    done = pltpu.make_async_copy(
-        new_ref, out_ref.at[pl.ds(odd * (planes - DEPTH), DEPTH)], sem
-    )
-    done.start()
-    done.wait()
+    nearest = copy(0, 1, sem.at[0])
+    nearest.start()
+    outer.wait()
+    nearest.wait()
 
 
 def shape(*dims):
@@ -474,7 +483,6 @@
             pltpu.SemaphoreType.DMA,
         ],
         compiler_params=PARAMS,
-        cost_estimate=HEAVY,
     )(facts, distribution, low, high, outer, inner, inner_halo, coef, cell)
 
     return pl.pallas_call(
@@ -486,7 +494,7 @@
             pltpu.VMEM((DEPTH, *block), jnp.float32),
             pltpu.VMEM(block, jnp.float32),
             pltpu.VMEM(block, jnp.float32),
-            pltpu.SemaphoreType.DMA,
+            pltpu.SemaphoreType.DMA((2,)),
         ],
         input_output_aliases={6: 0},
         compiler_params=PARAMS,

time: 69.3 us -> 68.9 us (level)
  no operation moved by 1% of the time
where the time goes in v3:
time: 68.9 us; the launch traced here: 68.6 us
  starting transfers between devices  32.1 us (47%)
  waiting for transfers between devices  20 us (29%)
  Pallas kernels  14.8 us (21%)
  local copies, waits for them, and re-layouts  1.5 us (2%)
    ppermute x1, waiting for transfers between devices, shards(): total = part + lax.ppermute(part, 'vz', opposite)  15 us
    pallas_call x1, Pallas kernels, shards(): pl.pallas_call(main_kernel, out_shape=[shape(planes, *block), shape(4, *b...  10.1 us
    ppermute x1, starting transfers between devices, shards(): total = part + lax.ppermute(part, 'vz', opposite)  9.6 us
    ppermute x2, starting transfers between devices, both_ways(): lax.ppermute(down, 'space', backward)  7.73 us
    ppermute x2, starting transfers between devices, both_ways(): lax.ppermute(up, 'space', forward)  7.1 us
    ppermute x1, waiting for transfers between devices, shards(): outer_halo = lax.ppermute(outer, 'vz', crossing)  4.16 us
    ppermute x1, starting transfers between devices, shards(): outer_halo = lax.ppermute(outer, 'vz', crossing)  2.93 us
    ppermute x1, starting transfers between devices, shards(): part = part + lax.ppermute(part, 'vz', partners)  2.85 us
  transfers between devices with their start and end apart: 8, of which 3 were waited for; matrix products, arithmetic and copies ran while one was open for 0% of the time, Pallas kernels for 18%

profile of v3, /device:TPU:69, one launch (start us, length us, event | category | flops | bytes accessed | tf_op | source)
XLA Modules:
  0.0 68.6 jit_solution(17522063673045152179)
XLA Ops:
  0.0 0.0 copy-start
  0.0 1.4 %slice.9 = f32[2,3,2,8,2304]{4,3,2,1,0:T(8,128)S(1)} slice(f32[4,3,2,8,2304]{4,3,2,1,0:T(8,128)} %bitcast.4), slice={[0:4:3], [0:3:1], [0:2:1], [0:8:1], [0:2304:1]} | slice | bytes 1769472 | tf_op jit(solution)/shard_map/slice | solution.py:429
  1.4 0.1 fusion
  1.4 4.0 %collective-permute-start = (f32[6,2,8,1152]{3,2,1,0:T(8,128)S(1)}, f32[6,2,8,1152]{3,2,1,0:T(8,128)S(1)}, u32[]{:S(2)}, u32[]{:S(2)}) collective-permute-start(f32[6,2,8,1152]{3,2,1,0:T(8,128)S(1)} %bitcast.6), channel_id=1, source_target_pairs={{0,4},{4,8},{8,12},{12,16},{16,20},{20,24},{24,28},{28,32},{32,36}... | collective-permute-start | bytes 1327112 | tf_op jit(solution)/shard_map/ppermute | solution.py:426
  5.4 1.9 %collective-permute-start.1 = (f32[6,2,8,1152]{3,2,1,0:T(8,128)S(1)}, f32[6,2,8,1152]{3,2,1,0:T(8,128)S(1)}, u32[]{:S(2)}, u32[]{:S(2)}) collective-permute-start(f32[6,2,8,1152]{3,2,1,0:T(8,128)S(1)} %bitcast.5), channel_id=1, source_target_pairs={{4,0},{8,4},{12,8},{16,12},{20,16},{24,20},{28,24},{32,28},{36,32}... | collective-permute-start | bytes 1327112 | tf_op jit(solution)/shard_map/ppermute | solution.py:426
  7.4 0.1 pad_add_fusion.slab_ref
  7.4 0.0 copy-done
  7.5 1.0 %shard_map.28 = (f32[2,8,128]{2,1,0:T(8,128)S(1)}, f32[6,2,8,1152]{3,2,1,0:T(8,128)S(1)}, f32[6,2,8,1152]{3,2,1,0:T(8,128)S(1)}) custom-call(s32[2]{0:T(128)S(1)} %pad_add_fusion.slab_ref, f32[12,2,8,2304]{3,2,1,0:T(8,128)S(1)} %copy-done), custom_call_target="tpu_custom_call" | custom-call | tf_op jit(solution)/shard_map/pallas_call | solution.py:437
  8.5 2.9 %collective-permute-start.2 = (f32[2,8,128]{2,1,0:T(8,128)S(1)}, f32[2,8,128]{2,1,0:T(8,128)S(1)}, u32[]{:S(2)}, u32[]{:S(2)}) collective-permute-start(f32[2,8,128]{2,1,0:T(8,128)S(1)} %get-tuple-element.22), channel_id=1, source_target_pairs={{0,1},{1,0},{2,3},{3,2},{4,5},{5,4},{6,7},{7,6},{8,9},{9,8},{10,11... | collective-permute-start | bytes 24584 | tf_op jit(solution)/shard_map/ppermute | solution.py:445
  11.3 0.8 %collective-permute-done.2 = f32[2,8,128]{2,1,0:T(8,128)S(1)} collective-permute-done((f32[2,8,128]{2,1,0:T(8,128)S(1)}, f32[2,8,128]{2,1,0:T(8,128)S(1)}, u32[]{:S(2)}, u32[]{:S(2)}) %collective-permute-start.2) | collective-permute-done | bytes 8224 | tf_op jit(solution)/shard_map/ppermute | solution.py:445
  12.1 9.6 %collective-permute-start.7 = (f32[2,8,128]{2,1,0:T(8,128)S(1)}, f32[2,8,128]{2,1,0:T(8,128)S(1)}, u32[]{:S(2)}, u32[]{:S(2)}) collective-permute-start(f32[2,8,128]{2,1,0:T(8,128)S(1)} %add.6), channel_id=1, source_target_pairs={{0,3},{1,2},{2,1},{3,0},{4,7},{5,6},{6,5},{7,4},{8,11},{9,10},{10,... | collective-permute-start | bytes 24584 | tf_op jit(solution)/shard_map/ppermute | solution.py:447
  21.7 3.1 %collective-permute-start.4 = (f32[6,2,8,1152]{3,2,1,0:T(8,128)S(1)}, f32[6,2,8,1152]{3,2,1,0:T(8,128)S(1)}, u32[]{:S(2)}, u32[]{:S(2)}) collective-permute-start(f32[6,2,8,1152]{3,2,1,0:T(8,128)S(1)} %get-tuple-element.26), channel_id=1, source_target_pairs={{0,4},{4,8},{8,12},{12,16},{16,20},{20,24},{24,28},{28,32},{32,36}... | collective-permute-start | bytes 1327112 | tf_op jit(solution)/shard_map/ppermute | solution.py:426
  24.8 5.8 %collective-permute-start.5 = (f32[6,2,8,1152]{3,2,1,0:T(8,128)S(1)}, f32[6,2,8,1152]{3,2,1,0:T(8,128)S(1)}, u32[]{:S(2)}, u32[]{:S(2)}) collective-permute-start(f32[6,2,8,1152]{3,2,1,0:T(8,128)S(1)} %get-tuple-element.27), channel_id=1, source_target_pairs={{4,0},{8,4},{12,8},{16,12},{20,16},{24,20},{28,24},{32,28},{36,32}... | collective-permute-start | bytes 1327112 | tf_op jit(solution)/shard_map/ppermute | solution.py:426
  30.7 15.0 %collective-permute-done.7 = f32[2,8,128]{2,1,0:T(8,128)S(1)} collective-permute-done((f32[2,8,128]{2,1,0:T(8,128)S(1)}, f32[2,8,128]{2,1,0:T(8,128)S(1)}, u32[]{:S(2)}, u32[]{:S(2)}) %collective-permute-start.7) | collective-permute-done | bytes 8224 | tf_op jit(solution)/shard_map/ppermute | solution.py:447
  45.7 0.0 copy-start.1
  45.7 0.0 collective-permute-done.low_ref
  45.7 0.0 collective-permute-done.1.high_ref
  45.7 1.2 %shard_map.29 = (f32[3,2,8,2304]{3,2,1,0:T(8,128)S(1)}, f32[3,2,8,2304]{3,2,1,0:T(8,128)S(1)}) custom-call(s32[2]{0:T(128)S(1)} %pad_add_fusion.slab_ref, f32[12,2,8,2304]{3,2,1,0:T(8,128)S(1)} %copy-done, f32[6,2,8,1152]{3,2,1,0:T(8,128)S(1)} %collective-permute-done.low_ref, f32[6,2,8,1152]{3,2,1,0:T(8,128)S(1)} %collective-permute-done.1.high_ref), custom_call_target="tpu_custom_call" | custom-call | flops 20000000000 | bytes 20000000 | tf_op jit(solution)/shard_map/pallas_call | solution.py:449
  46.9 1.9 %collective-permute-start.6 = (f32[3,2,8,2304]{3,2,1,0:T(8,128)S(1)}, f32[3,2,8,2304]{3,2,1,0:T(8,128)S(1)}, u32[]{:S(2)}, u32[]{:S(2)}) collective-permute-start(f32[3,2,8,2304]{3,2,1,0:T(8,128)S(1)} %get-tuple-element.28.inner_ref), channel_id=1, source_target_pairs={{0,1},{1,0},{2,3},{3,2},{4,5},{5,4},{6,7},{7,6},{8,9},{9,8},{10,11... | collective-permute-start | bytes 1327112 | tf_op jit(solution)/shard_map/ppermute | solution.py:459
  48.8 2.9 %collective-permute-start.3 = (f32[3,2,8,2304]{3,2,1,0:T(8,128)S(1)}, f32[3,2,8,2304]{3,2,1,0:T(8,128)S(1)}, u32[]{:S(2)}, u32[]{:S(2)}) collective-permute-start(f32[3,2,8,2304]{3,2,1,0:T(8,128)S(1)} %get-tuple-element.25.outer_ref), channel_id=1, source_target_pairs={{1,2},{2,1},{5,6},{6,5},{9,10},{10,9},{13,14},{14,13},{17,18},{18,... | collective-permute-start | bytes 1327112 | tf_op jit(solution)/shard_map/ppermute | solution.py:458
  51.8 0.0 copy-done.1
  51.8 0.1 broadcast_in_dim.2.rate_ref
  51.8 0.2 shard_map.30
  52.1 0.0 collective-permute-done.4.low_ref
  52.1 0.0 collective-permute-done.5.high_ref
  52.1 0.0 collective-permute-done.6.halo_ref
  52.1 10.1 %shard_map.31 = (f32[12,2,8,2304]{3,2,1,0:T(8,128)}, f32[4,2,8,2304]{3,2,1,0:T(8,128)S(1)}) custom-call(s32[2]{0:T(128)S(1)} %pad_add_fusion.slab_ref, f32[12,2,8,2304]{3,2,1,0:T(8,128)S(1)} %copy-done, f32[6,2,8,1152]{3,2,1,0:T(8,128)S(1)} %collective-permute-done.4.low_ref, f32[6,2,8,1152]{3,2,1,0:T(8,128)S(1)} %collective-permute-done.5.high_ref, ...), custom_call_target="tpu_custom_call" | custom-call | tf_op jit(solution)/shard_map/pallas_call | solution.py:471
  62.2 4.2 %collective-permute-done.3.halo_ref = f32[3,2,8,2304]{3,2,1,0:T(8,128)S(1)} collective-permute-done((f32[3,2,8,2304]{3,2,1,0:T(8,128)S(1)}, f32[3,2,8,2304]{3,2,1,0:T(8,128)S(1)}, u32[]{:S(2)}, u32[]{:S(2)}) %collective-permute-start.3) | collective-permute-done | bytes 442400 | tf_op jit(solution)/shard_map/ppermute | solution.py:458
  66.4 2.2 %shard_map.32 = f32[12,2,8,2304]{3,2,1,0:T(8,128)} custom-call(s32[2]{0:T(128)S(1)} %pad_add_fusion.slab_ref, f32[3,2,8,2304]{3,2,1,0:T(8,128)S(1)} %collective-permute-done.3.halo_ref, f32[3,2,8,2304]{3,2,1,0:T(8,128)S(1)} %get-tuple-element.25.outer_ref, f32[4,2,8,2304]{3,2,1,0:T(8,128)S(1)} %get-tuple-element.31.kept_ref, ...), custom_call_target="tpu_custom_call", output_to_operand_aliasing={{}: (6, {})} | custom-call | tf_op jit(solution)/shard_map/pallas_call | solution.py:488
  (2 shorter events, 0.0 us)
Async XLA Ops:
  0.0 7.4 %copy-start = (f32[12,2,8,2304]{3,2,1,0:T(8,128)S(1)}, f32[12,2,8,2304]{3,2,1,0:T(8,128)}, u32[]{:S(2)}) copy-start(f32[12,2,8,2304]{3,2,1,0:T(8,128)} %f_ref.4) | copy-start | bytes 5308420
  1.4 44.3 %collective-permute-start = (f32[6,2,8,1152]{3,2,1,0:T(8,128)S(1)}, f32[6,2,8,1152]{3,2,1,0:T(8,128)S(1)}, u32[]{:S(2)}, u32[]{:S(2)}) collective-permute-start(f32[6,2,8,1152]{3,2,1,0:T(8,128)S(1)} %bitcast.6), channel_id=1, source_target_pairs={{0,4},{4,8},{8,12},{12,16},{16,20},{20,24},{24,28},{28,32},{32,36}... | collective-permute-start | bytes 1327112 | tf_op jit(solution)/shard_map/ppermute | solution.py:426
  5.4 40.3 %collective-permute-start.1 = (f32[6,2,8,1152]{3,2,1,0:T(8,128)S(1)}, f32[6,2,8,1152]{3,2,1,0:T(8,128)S(1)}, u32[]{:S(2)}, u32[]{:S(2)}) collective-permute-start(f32[6,2,8,1152]{3,2,1,0:T(8,128)S(1)} %bitcast.5), channel_id=1, source_target_pairs={{4,0},{8,4},{12,8},{16,12},{20,16},{24,20},{28,24},{32,28},{36,32}... | collective-permute-start | bytes 1327112 | tf_op jit(solution)/shard_map/ppermute | solution.py:426
  8.5 3.7 %collective-permute-start.2 = (f32[2,8,128]{2,1,0:T(8,128)S(1)}, f32[2,8,128]{2,1,0:T(8,128)S(1)}, u32[]{:S(2)}, u32[]{:S(2)}) collective-permute-start(f32[2,8,128]{2,1,0:T(8,128)S(1)} %get-tuple-element.22), channel_id=1, source_target_pairs={{0,1},{1,0},{2,3},{3,2},{4,5},{5,4},{6,7},{7,6},{8,9},{9,8},{10,11... | collective-permute-start | bytes 24584 | tf_op jit(solution)/shard_map/ppermute | solution.py:445
  12.1 33.5 %collective-permute-start.7 = (f32[2,8,128]{2,1,0:T(8,128)S(1)}, f32[2,8,128]{2,1,0:T(8,128)S(1)}, u32[]{:S(2)}, u32[]{:S(2)}) collective-permute-start(f32[2,8,128]{2,1,0:T(8,128)S(1)} %add.6), channel_id=1, source_target_pairs={{0,3},{1,2},{2,1},{3,0},{4,7},{5,6},{6,5},{7,4},{8,11},{9,10},{10,... | collective-permute-start | bytes 24584 | tf_op jit(solution)/shard_map/ppermute | solution.py:447
  21.7 30.3 %collective-permute-start.4 = (f32[6,2,8,1152]{3,2,1,0:T(8,128)S(1)}, f32[6,2,8,1152]{3,2,1,0:T(8,128)S(1)}, u32[]{:S(2)}, u32[]{:S(2)}) collective-permute-start(f32[6,2,8,1152]{3,2,1,0:T(8,128)S(1)} %get-tuple-element.26), channel_id=1, source_target_pairs={{0,4},{4,8},{8,12},{12,16},{16,20},{20,24},{24,28},{28,32},{32,36}... | collective-permute-start | bytes 1327112 | tf_op jit(solution)/shard_map/ppermute | solution.py:426
  24.8 27.2 %collective-permute-start.5 = (f32[6,2,8,1152]{3,2,1,0:T(8,128)S(1)}, f32[6,2,8,1152]{3,2,1,0:T(8,128)S(1)}, u32[]{:S(2)}, u32[]{:S(2)}) collective-permute-start(f32[6,2,8,1152]{3,2,1,0:T(8,128)S(1)} %get-tuple-element.27), channel_id=1, source_target_pairs={{4,0},{8,4},{12,8},{16,12},{20,16},{24,20},{28,24},{32,28},{36,32}... | collective-permute-start | bytes 1327112 | tf_op jit(solution)/shard_map/ppermute | solution.py:426
  45.7 6.1 %copy-start.1 = (f32[2,8]{1,0:T(2,128)S(1)}, f32[2,8]{1,0:T(2,128)}, u32[]{:S(2)}) copy-start(f32[2,8]{1,0:T(2,128)} %param.3) | copy-start | bytes 196
  46.9 5.2 %collective-permute-start.6 = (f32[3,2,8,2304]{3,2,1,0:T(8,128)S(1)}, f32[3,2,8,2304]{3,2,1,0:T(8,128)S(1)}, u32[]{:S(2)}, u32[]{:S(2)}) collective-permute-start(f32[3,2,8,2304]{3,2,1,0:T(8,128)S(1)} %get-tuple-element.28.inner_ref), channel_id=1, source_target_pairs={{0,1},{1,0},{2,3},{3,2},{4,5},{5,4},{6,7},{7,6},{8,9},{9,8},{10,11... | collective-permute-start | bytes 1327112 | tf_op jit(solution)/shard_map/ppermute | solution.py:459
  48.8 17.6 %collective-permute-start.3 = (f32[3,2,8,2304]{3,2,1,0:T(8,128)S(1)}, f32[3,2,8,2304]{3,2,1,0:T(8,128)S(1)}, u32[]{:S(2)}, u32[]{:S(2)}) collective-permute-start(f32[3,2,8,2304]{3,2,1,0:T(8,128)S(1)} %get-tuple-element.25.outer_ref), channel_id=1, source_target_pairs={{1,2},{2,1},{5,6},{6,5},{9,10},{10,9},{13,14},{14,13},{17,18},{18,... | collective-permute-start | bytes 1327112 | tf_op jit(solution)/shard_map/ppermute | solution.py:458
